TPU v7x, 32 devices: a whole 2x2x4 slice. The times are simulated.
32 devices in a mesh: replica: 1, adapter: 32 (over z, y, x, core), tensor: 1.
Axes of the slice: x: 2, y: 2, z: 4, core: 2. Of those that a mesh axis runs over, the one named last changes fastest.
Arguments:
- hidden: bfloat16 [2, 8192, 8192], P(None, ('replica', 'adapter'), 'tensor'), may hold values from -6 to 6
- request_adapter_index: int32 [8192, 1], P(('replica', 'adapter')), may hold values from 0 to 127; in each aligned block of 256 rows (0 to 255, 256 to 511, ...) at most 2 rows name the same one
- key_base_weight: bfloat16 [8192, 1024], P('tensor'), may hold values from -0.0625 to 0.0625
- adapter_down_weight: bfloat16 [128, 8192, 64], P('adapter', 'tensor'), may hold values from -0.0625 to 0.0625
- adapter_up_weight: bfloat16 [128, 64, 1024], P('adapter', None, 'tensor'), may hold values from -0.75 to 0.75
Outputs:
- adapted_keys: bfloat16 [2, 8192, 1024], P(None, ('replica', 'adapter'), 'tensor')
Inputs may be any that keep to these rules, and one draw needn't show every extreme that they name: `request_adapter_index`: among the requests held by one device along `adapter`, no adapter is named more than 2 times.
All inputs are finite; a program needn't handle non-finite values.
Results may differ from a plain program's by a relative error of at most 0.005.
Values may be sent and summed in bfloat16 or wider, within the bound.
No kernel may reach another device: no remote copies, remote signals or barrier semaphores. Data moves between devices by JAX's collectives and lax.ppermute only.
A program may use at most 128 MiB of HBM per device.

v0:
```python
import jax
import jax.numpy as jnp
from jax import lax
from jax.sharding import PartitionSpec as P

MOST = 2


def per_device(
    hidden, request_adapter_index, key_base_weight, adapter_down_weight, adapter_up_weight
):
    step_count, req_rows, half_width = hidden.shape
    owners = lax.axis_size("adapter")
    local_request_count = adapter_down_weight.shape[0]
    adapter_table = owners * local_request_count
    adapter_rows = step_count * MOST
    selected_down = request_adapter_index[:, 0]
    position = jnp.arange(req_rows, dtype=jnp.int32)
    same_before = (selected_down[:, None] == selected_down[None, :]) & (
        position[None, :] < position[:, None]
    )
    earlier = jnp.sum(same_before.astype(jnp.int32), axis=1)
    step_index = jnp.arange(step_count, dtype=jnp.int32)
    slot_grid = (
        selected_down[None, :] * adapter_rows + earlier[None, :] * step_count + step_index[:, None]
    )
    adapter_slots = slot_grid.reshape(-1)
    flat_rows = hidden.reshape(step_count * req_rows, half_width)
    outgoing = (
        jnp.zeros((adapter_table * adapter_rows, half_width), jnp.bfloat16)
        .at[adapter_slots]
        .set(flat_rows)
    )
    outgoing = outgoing.reshape(owners, local_request_count, adapter_rows, half_width)
    partial_low = jnp.einsum(
        "sacd,adr->sacr",
        lax.all_to_all(outgoing, "adapter", split_axis=0, concat_axis=0, tiled=True),
        adapter_down_weight,
        preferred_element_type=jnp.float32,
    )
    summed = lax.psum(partial_low, "tensor")
    reduced_state = summed.astype(jnp.bfloat16)
    projected_keys = jnp.einsum(
        "dkbv,kvz->dkbz", reduced_state, adapter_up_weight, preferred_element_type=jnp.float32
    )
    result_keys = lax.all_to_all(
        projected_keys.astype(jnp.bfloat16), "adapter", split_axis=0, concat_axis=0, tiled=True
    )
    output_width = result_keys.shape[3]
    adapter_output = result_keys.reshape(adapter_table * adapter_rows, output_width)[adapter_slots]
    partial_value = jnp.dot(flat_rows, key_base_weight, preferred_element_type=jnp.float32)
    total = lax.psum(partial_value, "tensor")
    base_portion = lax.dynamic_slice_in_dim(
        total, lax.axis_index("tensor") * output_width, output_width, 1
    )
    adapted_keys = base_portion + adapter_output.astype(jnp.float32)
    return adapted_keys.reshape(step_count, req_rows, output_width).astype(jnp.bfloat16)


def solution(mesh):
    return jax.shard_map(
        per_device,
        mesh=mesh,
        in_specs=(
            P(None, ("replica", "adapter"), "tensor"),
            P(("replica", "adapter"), None),
            P("tensor", None),
            P("adapter", "tensor", None),
            P("adapter", None, "tensor"),
        ),
        out_specs=P(None, ("replica", "adapter"), "tensor"),
        check_vma=False,
    )
```

profile of v0, /device:TPU:1, one launch (start us, length us, event | category | flops | bytes accessed | tf_op | source)
XLA Modules:
  0.0 284.1 jit_solution(5135092351520904255)
XLA Ops:
  0.0 0.0 copy-start
  0.0 0.9 convert_reduce_fusion
  0.9 0.7 multiply_add_fusion
  1.6 18.6 %scatter_custom_fusion = bf16[512,8192]{1,0:T(8,128)(2,1)} fusion(s32[512]{0:T(512)S(1)} %bitcast.35, bf16[512,8192]{1,0:T(8,128)(2,1)} %bitcast.38, bf16[]{:T(256)} %constant.5.clone.1), kind=kCustom, calls=%fused_computation.5 | custom fusion | bytes 8389120 | tf_op jit(solution)/shard_map/scatter | solution.py:32
  20.3 13.1 %reshape.56 = bf16[32,4,4,8192]{3,2,1,0:T(4,128)(2,1)} reshape(bf16[512,8192]{1,0:T(8,128)(2,1)} %scatter_custom_fusion) | data formatting | bytes 16777216 | tf_op jit(solution)/shard_map/reshape | solution.py:34
  33.4 189.8 %all_to_all.10 = bf16[32,4,4,8192]{3,2,1,0:T(4,128)(2,1)} all-to-all(bf16[32,4,4,8192]{3,2,1,0:T(4,128)(2,1)} %reshape.56), channel_id=1, replica_groups=mesh['replica'=1,'adapter'=32,'tensor'=1] {'adapter'}, dimensions={0} | all-to-all | bytes 16777216 | tf_op jit(solution)/shard_map/all_to_all | solution.py:37
  223.2 0.0 copy-done
  223.2 10.9 %fusion.5 = bf16[32,4,4,1024]{3,0,2,1:T(8,128)(2,1)S(1)} fusion(bf16[4,8192,64]{1,2,0:T(8,128)(2,1)} %param.8, bf16[32,4,4,8192]{3,2,1,0:T(4,128)(2,1)} %all_to_all.10, bf16[4,64,1024]{2,1,0:T(8,128)(2,1)S(1)} %copy-done), kind=kOutput, calls=%fused_computation.9 | convolution fusion | flops 604536832 | bytes 14155776 | tf_op jit(solution)/shard_map/dkbv,kvz->dkbz/dot_general | solution.py:43
  234.2 1.8 copy.13
  235.9 4.8 %all-to-all-start.1 = ((bf16[32,4,4,1024]{3,2,1,0:T(4,128)(2,1)}), bf16[32,4,4,1024]{3,2,1,0:T(4,128)(2,1)S(1)}, u32[]{:S(2)}, u32[]{:S(2)}) async-start(bf16[32,4,4,1024]{3,2,1,0:T(4,128)(2,1)} %copy.13), calls=%async_computation.1 | async-start | bytes 2097152 | tf_op jit(solution)/shard_map/all_to_all | solution.py:46
  240.7 25.3 %all-to-all-done.1 = bf16[32,4,4,1024]{3,2,1,0:T(4,128)(2,1)S(1)} async-done(((bf16[32,4,4,1024]{3,2,1,0:T(4,128)(2,1)}), bf16[32,4,4,1024]{3,2,1,0:T(4,128)(2,1)S(1)}, u32[]{:S(2)}, u32[]{:S(2)}) %all-to-all-start.1) | async-done | bytes 1048608 | tf_op jit(solution)/shard_map/all_to_all | solution.py:46
  266.0 0.3 reshape.57
  266.3 2.1 gather_fusion
  268.4 15.7 %add_convert_fusion = bf16[512,1024]{1,0:T(8,128)(2,1)} fusion(bf16[512,1024]{1,0:T(8,128)(2,1)S(1)} %gather_fusion, bf16[512,8192]{1,0:T(8,128)(2,1)} %bitcast.39, bf16[8192,1024]{1,0:T(8,128)(2,1)} %param.7), kind=kOutput, calls=%fused_computation.7 | convolution fusion | flops 8591507456 | bytes 27262976 | tf_op jit(solution)/shard_map/dot_general | solution.py:51
  (4 shorter events, 0.0 us)
Async XLA Ops:
  0.0 223.2 %copy-start = (bf16[4,64,1024]{2,1,0:T(8,128)(2,1)S(1)}, bf16[4,64,1024]{2,1,0:T(8,128)(2,1)}, u32[]{:S(2)}) copy-start(bf16[4,64,1024]{2,1,0:T(8,128)(2,1)} %param.9) | copy-start | bytes 1572868
  235.9 30.1 %all-to-all-start.1 = ((bf16[32,4,4,1024]{3,2,1,0:T(4,128)(2,1)}), bf16[32,4,4,1024]{3,2,1,0:T(4,128)(2,1)S(1)}, u32[]{:S(2)}, u32[]{:S(2)}) async-start(bf16[32,4,4,1024]{3,2,1,0:T(4,128)(2,1)} %copy.13), calls=%async_computation.1 | async-start | bytes 2097152 | tf_op jit(solution)/shard_map/all_to_all | solution.py:46
where the time goes:
time: 286 us; the launch traced here: 284 us
  blocking collectives  190 us (66%)
  local copies, waits for them, and re-layouts  35.8 us (13%)
  matrix products  26.7 us (9%)
  waiting for transfers between devices  25.3 us (9%)
  starting transfers between devices  4.77 us (2%)
    all_to_all x1, blocking collectives, per_device(): lax.all_to_all(outgoing, 'adapter', split_axis=0, concat_axis=0, tiled=True)  190 us
    all_to_all x1, waiting for transfers between devices, per_device(): lax.all_to_all(projected_keys.astype(jnp.bfloat16), 'adapter', split_axis...  25.3 us
    scatter x1, local copies, waits for them, and re-layouts, per_device(): outgoing = jnp.zeros((adapter_table * adapter_rows, half_width), jnp.bflo...  18.6 us
    dot_general x1, matrix products, per_device(): jnp.dot(flat_rows, key_base_weight, preferred_element_type=jnp.float32)  15.7 us
    reshape x1, local copies, waits for them, and re-layouts, per_device(): outgoing.reshape(owners, local_request_count, adapter_rows, half_width)  13.1 us
    dot_general x1, matrix products, per_device(): jnp.einsum('dkbv,kvz->dkbz', reduced_state, adapter_up_weight, preferred_...  10.9 us
  transfers between devices with their start and end apart: 1, of which 1 were waited for; matrix products, arithmetic and copies ran while one was open for 0% of the time, Pallas kernels for 0%

commit v1 on v0

v1 whole, which is shorter than its diff:
```python
import functools

import jax
import jax.numpy as jnp
from jax import lax
from jax.experimental import pallas as pl
from jax.experimental.pallas import tpu as pltpu
from jax.sharding import PartitionSpec as P

MOST = 2
MIB = 1 << 20


def block_of(width, most):
    block = min(width, most)
    while width % block:
        block -= 128
    return block


def deal_kernel(steps, selected_ref, rows_ref, out_ref, deal_ref):
    requests = selected_ref.shape[1]
    slots = deal_ref.shape[0]

    @pl.when(pl.program_id(0) == 0)
    def _():
        selected = selected_ref[...]
        along = jnp.broadcast_to(selected, (requests, requests))
        first = lax.broadcasted_iota(jnp.int32, (requests, requests), 0)
        second = lax.broadcasted_iota(jnp.int32, (requests, requests), 1)
        down = jnp.sum(jnp.where(first == second, along, 0), axis=1, keepdims=True)
        before = (down == along) & (first < second)
        earlier = jnp.sum(before.astype(jnp.int32), axis=0, keepdims=True)
        start = (selected * MOST + earlier) * steps
        slot = lax.broadcasted_iota(jnp.int32, (slots, requests), 0)
        for step in range(steps):
            deal_ref[:, step * requests : (step + 1) * requests] = (
                (slot == start + step).astype(jnp.float32).astype(jnp.bfloat16)
            )

    out_ref[...] = jnp.dot(
        deal_ref[...], rows_ref[...], preferred_element_type=jnp.float32
    ).astype(jnp.bfloat16)


def deal_rows(selected, rows, steps, slots):
    count, width = rows.shape
    block = block_of(width, 1024)
    return pl.pallas_call(
        functools.partial(deal_kernel, steps),
        grid=(width // block,),
        in_specs=[
            pl.BlockSpec(selected.shape, lambda k: (0, 0)),
            pl.BlockSpec((count, block), lambda k: (0, k)),
        ],
        out_specs=pl.BlockSpec((slots, block), lambda k: (0, k)),
        out_shape=jax.ShapeDtypeStruct((slots, width), jnp.bfloat16),
        scratch_shapes=[pltpu.VMEM((slots, count), jnp.bfloat16)],
        compiler_params=pltpu.CompilerParams(vmem_limit_bytes=60 * MIB),
        cost_estimate=pl.CostEstimate(
            flops=2 * slots * count * width,
            bytes_accessed=2 * (slots + count) * width,
            transcendentals=0,
        ),
    )(selected, rows)


def own_columns(low, adapters, adapter_rows):
    rank = low.shape[1] // adapters
    row = lax.broadcasted_iota(jnp.int32, low.shape, 0)
    column = lax.broadcasted_iota(jnp.int32, low.shape, 1)
    own = (row // adapter_rows) % adapters == column // rank
    return jnp.where(own, low, 0.0).astype(jnp.bfloat16)


def term_kernel(adapters, adapter_rows, rows_ref, down_ref, up_ref, out_ref, low_ref):
    k = pl.program_id(0)

    @pl.when(k == 0)
    def _():
        low_ref[...] = jnp.zeros_like(low_ref)

    low_ref[...] += lax.dot_general(
        rows_ref[...],
        down_ref[...],
        (((1,), (0,)), ((), ())),
        preferred_element_type=jnp.float32,
    )

    @pl.when(k == pl.num_programs(0) - 1)
    def _():
        low = own_columns(low_ref[...], adapters, adapter_rows)
        out_ref[...] = jnp.dot(
            low, up_ref[...], preferred_element_type=jnp.float32
        ).astype(jnp.bfloat16)


def adapter_terms(rows, down, up, adapters, adapter_rows):
    slots, width = rows.shape
    ranks, out_width = up.shape
    block = block_of(width, 1024)
    return pl.pallas_call(
        functools.partial(term_kernel, adapters, adapter_rows),
        grid=(width // block,),
        in_specs=[
            pl.BlockSpec((slots, block), lambda k: (0, k)),
            pl.BlockSpec((block, ranks), lambda k: (k, 0)),
            pl.BlockSpec((ranks, out_width), lambda k: (0, 0)),
        ],
        out_specs=pl.BlockSpec((slots, out_width), lambda k: (0, 0)),
        out_shape=jax.ShapeDtypeStruct((slots, out_width), jnp.bfloat16),
        scratch_shapes=[pltpu.VMEM((slots, ranks), jnp.float32)],
        compiler_params=pltpu.CompilerParams(vmem_limit_bytes=60 * MIB),
        cost_estimate=pl.CostEstimate(
            flops=2 * slots * ranks * (width + out_width),
            bytes_accessed=2 * (slots + ranks) * (width + out_width),
            transcendentals=0,
        ),
    )(rows, down, up)


def finish_kernel(deal_ref, terms_ref, base_ref, out_ref):
    own = jnp.dot(deal_ref[...], terms_ref[...], preferred_element_type=jnp.float32)
    out_ref[...] = (base_ref[...] + own).astype(jnp.bfloat16)


def finish(deal_back, terms, base):
    return pl.pallas_call(
        finish_kernel,
        out_shape=jax.ShapeDtypeStruct(base.shape, jnp.bfloat16),
        compiler_params=pltpu.CompilerParams(vmem_limit_bytes=60 * MIB),
    )(deal_back, terms, base)


def per_device(
    hidden, request_adapter_index, key_base_weight, adapter_down_weight, adapter_up_weight
):
    steps, requests, width = hidden.shape
    owners = lax.axis_size("adapter")
    parts = lax.axis_size("tensor")
    adapters, _, rank = adapter_down_weight.shape
    out_width = adapter_up_weight.shape[2]
    adapter_rows = steps * MOST
    slots = owners * adapters * adapter_rows
    rows = hidden.reshape(steps * requests, width)
    selected = request_adapter_index.reshape(1, requests)

    outgoing = deal_rows(selected, rows, steps, slots)
    incoming = lax.all_to_all(outgoing, "adapter", split_axis=0, concat_axis=0, tiled=True)
    base = jnp.dot(rows, key_base_weight, preferred_element_type=jnp.float32)
    if parts > 1:
        base = lax.psum_scatter(base, "tensor", scatter_dimension=1, tiled=True)

    position = jnp.arange(requests, dtype=jnp.int32)
    before = (selected.T == selected) & (position[None, :] < position[:, None])
    earlier = jnp.sum(before.astype(jnp.int32), axis=1)
    start = (selected[0] * MOST + earlier) * steps
    slot = (start[None, :] + jnp.arange(steps, dtype=jnp.int32)[:, None]).reshape(-1)
    deal_back = (slot[:, None] == jnp.arange(slots, dtype=jnp.int32)[None, :]).astype(jnp.bfloat16)

    down = adapter_down_weight.transpose(1, 0, 2).reshape(width, adapters * rank)
    up = adapter_up_weight.reshape(adapters * rank, out_width)
    if parts > 1:
        low = jnp.dot(incoming, down, preferred_element_type=jnp.float32)
        low = own_columns(lax.psum(low, "tensor"), adapters, adapter_rows)
        terms = jnp.dot(low, up, preferred_element_type=jnp.float32).astype(jnp.bfloat16)
    else:
        terms = adapter_terms(incoming, down, up, adapters, adapter_rows)
    returned = lax.all_to_all(terms, "adapter", split_axis=0, concat_axis=0, tiled=True)
    out = finish(deal_back, returned, base)
    return out.reshape(steps, requests, out_width)


def solution(mesh):
    return jax.shard_map(
        per_device,
        mesh=mesh,
        in_specs=(
            P(None, ("replica", "adapter"), "tensor"),
            P(("replica", "adapter"), None),
            P("tensor", None),
            P("adapter", "tensor", None),
            P("adapter", None, "tensor"),
        ),
        out_specs=P(None, ("replica", "adapter"), "tensor"),
        check_vma=False,
    )
```

time: 286 us -> 249 us (0.87)
  blocking collectives: 190 us -> 0 us
  waiting for transfers between devices: 25.3 us -> 187 us
  local copies, waits for them, and re-layouts: 35.8 us -> 7.39 us
  Pallas kernels: 0 us -> 25 us
  matrix products: 26.7 us -> 15.9 us
  starting transfers between devices: 4.77 us -> 10.3 us
    all_to_all x1 -> x0, blocking collectives: 190 us -> none  [per_device(): lax.all_to_all(outgoing, 'adapter', split_axis=0, concat_axis=0, tiled=True)]
    all_to_all x1 -> x2, waiting for transfers between devices: 25.3 us -> 187 us  [the longest x1 178 us: per_device(): lax.all_to_all(outgoing, 'adapter', split_axis=0, concat_axis=0, tiled=True)]
    pallas_call x0 -> x3, Pallas kernels: none -> 25 us  [the longest x1 11.2 us: deal_rows(): pl.pallas_call(functools.partial(deal_kernel, steps), grid=(width // bloc...]
    scatter x1 -> x0, local copies, waits for them, and re-layouts: 18.6 us -> none  [per_device(): outgoing = jnp.zeros((adapter_table * adapter_rows, half_width), jnp.bflo...]
    dot_general x2 -> x1, matrix products: 26.7 us -> 15.9 us  [per_device(): base = jnp.dot(rows, key_base_weight, preferred_element_type=jnp.float32)]
    reshape x2 -> x1, local copies, waits for them, and re-layouts: 13.3 us -> 6.39 us  [per_device(): adapter_down_weight.transpose(1, 0, 2).reshape(width, adapters * rank)]
    all_to_all x1 -> x2, starting transfers between devices: 4.77 us -> 10.3 us  [the longest x1 7.15 us: per_device(): lax.all_to_all(outgoing, 'adapter', split_axis=0, concat_axis=0, tiled=True)]
  transfers between devices with their start and end apart: 1 -> 2, of which waited for: 1 -> 2; matrix products, arithmetic and copies ran while one was open for 0% -> 9% of each run, Pallas kernels for 0% -> 0%
where the time goes in v1:
time: 249 us; the launch traced here: 247 us
  waiting for transfers between devices  187 us (75%)
  Pallas kernels  25 us (10%)
  matrix products  15.9 us (6%)
  starting transfers between devices  10.3 us (4%)
  local copies, waits for them, and re-layouts  7.39 us (3%)
    all_to_all x1, waiting for transfers between devices, per_device(): lax.all_to_all(outgoing, 'adapter', split_axis=0, concat_axis=0, tiled=True)  178 us
    dot_general x1, matrix products, per_device(): base = jnp.dot(rows, key_base_weight, preferred_element_type=jnp.float32)  15.9 us
    pallas_call x1, Pallas kernels, deal_rows(): pl.pallas_call(functools.partial(deal_kernel, steps), grid=(width // bloc...  11.2 us
    pallas_call x1, Pallas kernels, adapter_terms(): pl.pallas_call(functools.partial(term_kernel, adapters, adapter_rows), gr...  9.99 us
    all_to_all x1, waiting for transfers between devices, per_device(): lax.all_to_all(terms, 'adapter', split_axis=0, concat_axis=0, tiled=True)  9.52 us
    all_to_all x1, starting transfers between devices, per_device(): lax.all_to_all(outgoing, 'adapter', split_axis=0, concat_axis=0, tiled=True)  7.15 us
    reshape x1, local copies, waits for them, and re-layouts, per_device(): adapter_down_weight.transpose(1, 0, 2).reshape(width, adapters * rank)  6.39 us
  transfers between devices with their start and end apart: 2, of which 2 were waited for; matrix products, arithmetic and copies ran while one was open for 9% of the time, Pallas kernels for 0%

profile of v1, /device:TPU:1, one launch (start us, length us, event | category | flops | bytes accessed | tf_op | source)
XLA Modules:
  0.0 247.2 jit_solution(4008904967234813040)
XLA Ops:
  0.0 11.2 %shard_map.55 = bf16[512,8192]{1,0:T(8,128)(2,1)} custom-call(s32[1,256]{1,0:T(1,128)} %bitcast.24, bf16[512,8192]{1,0:T(8,128)(2,1)} %bitcast.18), custom_call_target="tpu_custom_call" | custom-call | flops 4294967296 | bytes 16777216 | tf_op jit(solution)/shard_map/pallas_call | solution.py:49
  11.2 0.0 copy-start.1
  11.2 7.2 %all-to-all-start = ((bf16[32,16,8192]{2,1,0:T(8,128)(2,1)}), bf16[32,16,8192]{2,1,0:T(8,128)(2,1)}, u32[]{:S(2)}, u32[]{:S(2)}) async-start(bf16[32,16,8192]{2,1,0:T(8,128)(2,1)} %bitcast.17), calls=%async_computation | async-start | bytes 16777216 | tf_op jit(solution)/shard_map/all_to_all | solution.py:149
  18.4 0.0 copy-done.1
  18.4 0.2 convert_reduce_fusion
  18.6 6.4 %copy.8.down_ref = bf16[8192,256]{1,0:T(8,128)(2,1)} copy(bf16[8192,256]{0,1:T(8,128)(2,1)} %bitcast.21) | data formatting | bytes 8388608 | tf_op jit(solution)/shard_map/reshape | solution.py:161
  25.0 0.9 fusion.deal_ref
  25.9 177.9 %all-to-all-done = bf16[32,16,8192]{2,1,0:T(8,128)(2,1)} async-done(((bf16[32,16,8192]{2,1,0:T(8,128)(2,1)}), bf16[32,16,8192]{2,1,0:T(8,128)(2,1)}, u32[]{:S(2)}, u32[]{:S(2)}) %all-to-all-start) | async-done | bytes 8388640 | tf_op jit(solution)/shard_map/all_to_all | solution.py:149
  203.9 10.0 %shard_map.56 = bf16[512,1024]{1,0:T(8,128)(2,1)} custom-call(bf16[512,8192]{1,0:T(8,128)(2,1)} %bitcast.4.rows_ref, bf16[8192,256]{1,0:T(8,128)(2,1)} %copy.8.down_ref, bf16[256,1024]{1,0:T(8,128)(2,1)} %bitcast.23), custom_call_target="tpu_custom_call" | custom-call | flops 2415919104 | bytes 14155776 | tf_op jit(solution)/shard_map/pallas_call | solution.py:102
  213.9 3.1 %all-to-all-start.1 = ((bf16[32,16,1024]{2,1,0:T(8,128)(2,1)}), bf16[32,16,1024]{2,1,0:T(8,128)(2,1)S(1)}, u32[]{:S(2)}, u32[]{:S(2)}) async-start(bf16[32,16,1024]{2,1,0:T(8,128)(2,1)} %bitcast.20), calls=%async_computation.1 | async-start | bytes 2097152 | tf_op jit(solution)/shard_map/all_to_all | solution.py:169
  217.0 15.9 %fusion.2.base_ref = f32[512,1024]{1,0:T(8,128)} fusion(bf16[512,8192]{1,0:T(8,128)(2,1)} %bitcast.19, bf16[8192,1024]{1,0:T(8,128)(2,1)} %param.7), kind=kOutput, calls=%fused_computation.7 | convolution fusion | flops 8589934592 | bytes 27262976 | tf_op jit(solution)/shard_map/dot_general | solution.py:150
  232.9 9.5 %all-to-all-done.1 = bf16[32,16,1024]{2,1,0:T(8,128)(2,1)S(1)} async-done(((bf16[32,16,1024]{2,1,0:T(8,128)(2,1)}), bf16[32,16,1024]{2,1,0:T(8,128)(2,1)S(1)}, u32[]{:S(2)}, u32[]{:S(2)}) %all-to-all-start.1) | async-done | bytes 1048608 | tf_op jit(solution)/shard_map/all_to_all | solution.py:169
  242.5 0.0 copy-start
  242.5 1.0 copy-done
  243.5 3.8 %shard_map.57 = bf16[512,1024]{1,0:T(8,128)(2,1)} custom-call(bf16[512,512]{1,0:T(8,128)(2,1)} %fusion.deal_ref, bf16[512,1024]{1,0:T(8,128)(2,1)} %bitcast.22, f32[512,1024]{1,0:T(8,128)} %fusion.2.base_ref), custom_call_target="tpu_custom_call" | custom-call | tf_op jit(solution)/shard_map/pallas_call | solution.py:128
  (3 shorter events, 0.0 us)
Async XLA Ops:
  11.2 7.2 %copy-start.1 = (s32[256,1]{0,1:T(1,128)S(1)}, s32[256,1]{0,1:T(1,128)}, u32[]{:S(2)}) copy-start(s32[256,1]{0,1:T(1,128)} %param.6) | copy-start | bytes 3076
  11.2 192.7 %all-to-all-start = ((bf16[32,16,8192]{2,1,0:T(8,128)(2,1)}), bf16[32,16,8192]{2,1,0:T(8,128)(2,1)}, u32[]{:S(2)}, u32[]{:S(2)}) async-start(bf16[32,16,8192]{2,1,0:T(8,128)(2,1)} %bitcast.17), calls=%async_computation | async-start | bytes 16777216 | tf_op jit(solution)/shard_map/all_to_all | solution.py:149
  213.9 28.6 %all-to-all-start.1 = ((bf16[32,16,1024]{2,1,0:T(8,128)(2,1)}), bf16[32,16,1024]{2,1,0:T(8,128)(2,1)S(1)}, u32[]{:S(2)}, u32[]{:S(2)}) async-start(bf16[32,16,1024]{2,1,0:T(8,128)(2,1)} %bitcast.20), calls=%async_computation.1 | async-start | bytes 2097152 | tf_op jit(solution)/shard_map/all_to_all | solution.py:169
  242.5 1.0 copy-start

commit v2 on v1

v2 whole, which is shorter than its diff:
```python
import functools

import jax
import jax.numpy as jnp
from jax import lax
from jax.experimental import pallas as pl
from jax.experimental.pallas import tpu as pltpu
from jax.sharding import PartitionSpec as P

MOST = 2
MIB = 1 << 20


def block_of(width, most):
    block = min(width, most)
    while width % block:
        block -= 128
    return block


def deal_kernel(owners, block, selected_ref, rows_ref, out_ref, in_buf, out_buf, in_sem, out_sem):
    requests = selected_ref.shape[1]
    count, width = rows_ref.shape
    chunks = width // block
    steps = count // requests
    slots = out_ref.shape[0] // steps

    def load(k):
        part = pl.ds(k * block, block)
        return pltpu.make_async_copy(rows_ref.at[:, part], in_buf.at[:, part], in_sem.at[k])

    def store(k):
        part = pl.ds(k * block, block)
        return pltpu.make_async_copy(out_buf.at[:, part], out_ref.at[:, part], out_sem.at[k])

    for k in range(chunks):
        load(k).start()

    selected = selected_ref[...]
    along = jnp.broadcast_to(selected, (requests, requests))
    first = lax.broadcasted_iota(jnp.int32, (requests, requests), 0)
    second = lax.broadcasted_iota(jnp.int32, (requests, requests), 1)
    down = jnp.sum(jnp.where(first == second, along, 0), axis=1, keepdims=True)
    before = (down == along) & (first < second)
    earlier = jnp.sum(before.astype(jnp.int32), axis=0, keepdims=True)
    slot = lax.broadcasted_iota(jnp.int32, (slots, requests), 0)
    deal = (slot == selected * MOST + earlier).astype(jnp.float32).astype(jnp.bfloat16)

    for k in range(chunks):
        load(k).wait()
        part = slice(k * block, (k + 1) * block)
        dealt = [
            jnp.dot(
                deal,
                in_buf[step * requests : (step + 1) * requests, part],
                preferred_element_type=jnp.float32,
            ).reshape(owners, slots // owners, block)
            for step in range(steps)
        ]
        out_buf[:, part] = (
            jnp.concatenate(dealt, axis=1).reshape(slots * steps, block).astype(jnp.bfloat16)
        )
        store(k).start()
    for k in range(chunks):
        store(k).wait()


def deal_rows(selected, rows, owners, steps, slots):
    count, width = rows.shape
    block = block_of(width, 2048)
    return pl.pallas_call(
        functools.partial(deal_kernel, owners, block),
        in_specs=[
            pl.BlockSpec(memory_space=pltpu.VMEM),
            pl.BlockSpec(memory_space=pltpu.HBM),
        ],
        out_specs=pl.BlockSpec(memory_space=pltpu.HBM),
        out_shape=jax.ShapeDtypeStruct((slots, width), jnp.bfloat16),
        scratch_shapes=[
            pltpu.VMEM((count, width), jnp.bfloat16),
            pltpu.VMEM((slots, width), jnp.bfloat16),
            pltpu.SemaphoreType.DMA((width // block,)),
            pltpu.SemaphoreType.DMA((width // block,)),
        ],
        compiler_params=pltpu.CompilerParams(vmem_limit_bytes=60 * MIB),
        cost_estimate=pl.CostEstimate(
            flops=2 * slots * count * width // steps,
            bytes_accessed=2 * (slots + count) * width,
            transcendentals=0,
        ),
    )(selected, rows)


def own_columns(low, adapters):
    rank = low.shape[1] // adapters
    row = lax.broadcasted_iota(jnp.int32, low.shape, 0)
    column = lax.broadcasted_iota(jnp.int32, low.shape, 1)
    own = (row // MOST) % adapters == column // rank
    return jnp.where(own, low, 0.0).astype(jnp.bfloat16)


def term_kernel(
    adapters,
    parts,
    rows_ref,
    down_ref,
    up_ref,
    out_ref,
    rows_buf,
    down_buf,
    up_buf,
    low_ref,
    out_buf,
    rows_sem,
    down_sem,
    up_sem,
    out_sem,
):
    count = rows_ref.shape[0]
    block = count // out_sem.shape[0]
    last = len(parts) - 1

    def load(k):
        part = pl.ds(*parts[k])
        return (
            pltpu.make_async_copy(down_ref.at[part], down_buf.at[part], down_sem.at[k]),
            pltpu.make_async_copy(rows_ref.at[:, part], rows_buf.at[:, part], rows_sem.at[k]),
        )

    def store(i):
        part = pl.ds(i * block, block)
        return pltpu.make_async_copy(out_buf.at[part], out_ref.at[part], out_sem.at[i])

    load_up = pltpu.make_async_copy(up_ref, up_buf, up_sem)
    for k in range(last + 1):
        for copy in load(k):
            copy.start()
    load_up.start()
    for k, (start, size) in enumerate(parts):
        for copy in load(k):
            copy.wait()
        if k == last:
            load_up.wait()
        for i in range(count // block):
            part = slice(i * block, (i + 1) * block)
            low = jnp.dot(
                rows_buf[part, start : start + size],
                down_buf[start : start + size],
                preferred_element_type=jnp.float32,
            )
            if k > 0:
                low += low_ref[part]
            if k < last:
                low_ref[part] = low
                continue
            out_buf[part] = jnp.dot(
                own_columns(low, adapters), up_buf[...], preferred_element_type=jnp.float32
            ).astype(jnp.bfloat16)
            store(i).start()
    for i in range(count // block):
        store(i).wait()


def adapter_terms(rows, down, up, adapters):
    slots, width = rows.shape
    ranks, out_width = up.shape
    if width % 1024 == 0:
        eighths = (2, 3, 2, 1)
        ends = [sum(eighths[: k + 1]) * width // 8 for k in range(4)]
        parts = [(end - n * width // 8, n * width // 8) for end, n in zip(ends, eighths)]
    else:
        parts = [(0, width)]
    return pl.pallas_call(
        functools.partial(term_kernel, adapters, parts),
        in_specs=[pl.BlockSpec(memory_space=pltpu.HBM)] * 3,
        out_specs=pl.BlockSpec(memory_space=pltpu.HBM),
        out_shape=jax.ShapeDtypeStruct((slots, out_width), jnp.bfloat16),
        scratch_shapes=[
            pltpu.VMEM((slots, width), jnp.bfloat16),
            pltpu.VMEM((width, ranks), jnp.bfloat16),
            pltpu.VMEM((ranks, out_width), jnp.bfloat16),
            pltpu.VMEM((slots, ranks), jnp.float32),
            pltpu.VMEM((slots, out_width), jnp.bfloat16),
            pltpu.SemaphoreType.DMA((len(parts),)),
            pltpu.SemaphoreType.DMA((len(parts),)),
            pltpu.SemaphoreType.DMA,
            pltpu.SemaphoreType.DMA((2,)),
        ],
        compiler_params=pltpu.CompilerParams(vmem_limit_bytes=60 * MIB),
        cost_estimate=pl.CostEstimate(
            flops=2 * slots * ranks * (width + out_width),
            bytes_accessed=2 * (slots + ranks) * (width + out_width),
            transcendentals=0,
        ),
    )(rows, down, up)


def per_device(
    hidden, request_adapter_index, key_base_weight, adapter_down_weight, adapter_up_weight
):
    steps, requests, width = hidden.shape
    owners = lax.axis_size("adapter")
    parts = lax.axis_size("tensor")
    adapters, _, rank = adapter_down_weight.shape
    out_width = adapter_up_weight.shape[2]
    own_slots = adapters * MOST
    slots = owners * steps * own_slots
    rows = hidden.reshape(steps * requests, width)
    selected = request_adapter_index.reshape(1, requests)

    outgoing = deal_rows(selected, rows, owners, steps, slots)
    incoming = lax.all_to_all(outgoing, "adapter", split_axis=0, concat_axis=0, tiled=True)
    base = jnp.dot(rows, key_base_weight, preferred_element_type=jnp.float32)
    if parts > 1:
        base = lax.psum_scatter(base, "tensor", scatter_dimension=1, tiled=True)

    position = jnp.arange(requests, dtype=jnp.int32)
    before = (selected.T == selected) & (position[None, :] < position[:, None])
    earlier = jnp.sum(before.astype(jnp.int32), axis=1)
    place = selected[0] * MOST + earlier
    start = place // own_slots * (steps * own_slots) + place % own_slots
    slot = start[None, :] + jnp.arange(steps, dtype=jnp.int32)[:, None] * own_slots
    deal_back = slot.reshape(-1, 1) == jnp.arange(slots, dtype=jnp.int32)[None, :]
    deal_back = deal_back.astype(jnp.bfloat16)

    down = adapter_down_weight.transpose(1, 0, 2).reshape(width, adapters * rank)
    up = adapter_up_weight.reshape(adapters * rank, out_width)
    if parts > 1:
        low = jnp.dot(incoming, down, preferred_element_type=jnp.float32)
        low = own_columns(lax.psum(low, "tensor"), adapters)
        terms = jnp.dot(low, up, preferred_element_type=jnp.float32).astype(jnp.bfloat16)
    else:
        terms = adapter_terms(incoming, down, up, adapters)
    returned = lax.all_to_all(terms, "adapter", split_axis=0, concat_axis=0, tiled=True)
    base = lax.optimization_barrier(base)
    own = jnp.dot(deal_back, returned, preferred_element_type=jnp.float32)
    out = (base + own).astype(jnp.bfloat16)
    return out.reshape(steps, requests, out_width)


def solution(mesh):
    return jax.shard_map(
        per_device,
        mesh=mesh,
        in_specs=(
            P(None, ("replica", "adapter"), "tensor"),
            P(("replica", "adapter"), None),
            P("tensor", None),
            P("adapter", "tensor", None),
            P("adapter", None, "tensor"),
        ),
        out_specs=P(None, ("replica", "adapter"), "tensor"),
        check_vma=False,
    )
```

time: 249 us -> 238 us (0.956)
  Pallas kernels: 25 us -> 13.8 us
  waiting for transfers between devices: 187 us -> 190 us
    pallas_call x3 -> x2, Pallas kernels: 25 us -> 13.8 us  [the longest x1 7.05 us: adapter_terms(): pl.pallas_call(functools.partial(term_kernel, adapters, parts), in_specs=...]
where the time goes in v2:
time: 238 us; the launch traced here: 237 us
  waiting for transfers between devices  190 us (80%)
  matrix products  16 us (7%)
  Pallas kernels  13.8 us (6%)
  starting transfers between devices  10.3 us (4%)
  local copies, waits for them, and re-layouts  6.42 us (3%)
    all_to_all x1, waiting for transfers between devices, per_device(): lax.all_to_all(outgoing, 'adapter', split_axis=0, concat_axis=0, tiled=True)  179 us
    dot_general x1, matrix products, per_device(): base = jnp.dot(rows, key_base_weight, preferred_element_type=jnp.float32)  14.3 us
    all_to_all x1, waiting for transfers between devices, per_device(): lax.all_to_all(terms, 'adapter', split_axis=0, concat_axis=0, tiled=True)  11.1 us
    all_to_all x1, starting transfers between devices, per_device(): lax.all_to_all(outgoing, 'adapter', split_axis=0, concat_axis=0, tiled=True)  7.13 us
    pallas_call x1, Pallas kernels, adapter_terms(): pl.pallas_call(functools.partial(term_kernel, adapters, parts), in_specs=...  7.05 us
    pallas_call x1, Pallas kernels, deal_rows(): pl.pallas_call(functools.partial(deal_kernel, owners, block), in_specs=[p...  6.72 us
    reshape x1, local copies, waits for them, and re-layouts, per_device(): adapter_down_weight.transpose(1, 0, 2).reshape(width, adapters * rank)  6.41 us
  transfers between devices with their start and end apart: 2, of which 2 were waited for; matrix products, arithmetic and copies ran while one was open for 9% of the time, Pallas kernels for 0%

profile of v2, /device:TPU:1, one launch (start us, length us, event | category | flops | bytes accessed | tf_op | source)
XLA Modules:
  0.0 236.8 jit_solution(6182709048757690502)
XLA Ops:
  0.0 6.7 %shard_map.55 = bf16[512,8192]{1,0:T(8,128)(2,1)} custom-call(s32[1,256]{1,0:T(1,128)} %bitcast.25, bf16[512,8192]{1,0:T(8,128)(2,1)} %bitcast.19), custom_call_target="tpu_custom_call" | custom-call | flops 2147483648 | bytes 16777216 | tf_op jit(solution)/shard_map/pallas_call | solution.py:71
  6.7 0.0 copy-start
  6.7 7.1 %all-to-all-start = ((bf16[32,16,8192]{2,1,0:T(8,128)(2,1)}), bf16[32,16,8192]{2,1,0:T(8,128)(2,1)}, u32[]{:S(2)}, u32[]{:S(2)}) async-start(bf16[32,16,8192]{2,1,0:T(8,128)(2,1)} %bitcast.18), calls=%async_computation | async-start | bytes 16777216 | tf_op jit(solution)/shard_map/all_to_all | solution.py:212
  13.9 0.0 copy-done
  13.9 0.2 convert_reduce_fusion
  14.1 0.1 add_bitcast_fusion
  14.2 6.4 %copy.8.down_ref = bf16[8192,256]{1,0:T(8,128)(2,1)} copy(bf16[8192,256]{0,1:T(8,128)(2,1)} %bitcast.22) | data formatting | bytes 8388608 | tf_op jit(solution)/shard_map/reshape | solution.py:226
  20.6 178.8 %all-to-all-done = bf16[32,16,8192]{2,1,0:T(8,128)(2,1)} async-done(((bf16[32,16,8192]{2,1,0:T(8,128)(2,1)}), bf16[32,16,8192]{2,1,0:T(8,128)(2,1)}, u32[]{:S(2)}, u32[]{:S(2)}) %all-to-all-start) | async-done | bytes 8388640 | tf_op jit(solution)/shard_map/all_to_all | solution.py:212
  199.4 7.1 %shard_map.56 = bf16[512,1024]{1,0:T(8,128)(2,1)} custom-call(bf16[512,8192]{1,0:T(8,128)(2,1)} %bitcast.4.rows_ref, bf16[8192,256]{1,0:T(8,128)(2,1)} %copy.8.down_ref, bf16[256,1024]{1,0:T(8,128)(2,1)} %bitcast.24), custom_call_target="tpu_custom_call" | custom-call | flops 2415919104 | bytes 14155776 | tf_op jit(solution)/shard_map/pallas_call | solution.py:173
  206.5 3.1 %all-to-all-start.1 = ((bf16[32,16,1024]{2,1,0:T(8,128)(2,1)}), bf16[32,16,1024]{2,1,0:T(8,128)(2,1)S(1)}, u32[]{:S(2)}, u32[]{:S(2)}) async-start(bf16[32,16,1024]{2,1,0:T(8,128)(2,1)} %bitcast.21), calls=%async_computation.1 | async-start | bytes 2097152 | tf_op jit(solution)/shard_map/all_to_all | solution.py:234
  209.6 14.3 %fusion.3 = f32[512,1024]{1,0:T(8,128)S(1)} fusion(bf16[512,8192]{1,0:T(8,128)(2,1)} %bitcast.20, bf16[8192,1024]{1,0:T(8,128)(2,1)} %param.7), kind=kOutput, calls=%fused_computation.14 | convolution fusion | flops 8589934592 | bytes 27262976 | tf_op jit(solution)/shard_map/dot_general | solution.py:213
  223.9 11.1 %all-to-all-done.1 = bf16[32,16,1024]{2,1,0:T(8,128)(2,1)S(1)} async-done(((bf16[32,16,1024]{2,1,0:T(8,128)(2,1)}), bf16[32,16,1024]{2,1,0:T(8,128)(2,1)S(1)}, u32[]{:S(2)}, u32[]{:S(2)}) %all-to-all-start.1) | async-done | bytes 1048608 | tf_op jit(solution)/shard_map/all_to_all | solution.py:234
  235.0 1.7 add_convert_fusion
  (3 shorter events, 0.0 us)
Async XLA Ops:
  6.7 7.2 %copy-start = (s32[256,1]{0,1:T(1,128)S(1)}, s32[256,1]{0,1:T(1,128)}, u32[]{:S(2)}) copy-start(s32[256,1]{0,1:T(1,128)} %param.6) | copy-start | bytes 3076
  6.7 192.6 %all-to-all-start = ((bf16[32,16,8192]{2,1,0:T(8,128)(2,1)}), bf16[32,16,8192]{2,1,0:T(8,128)(2,1)}, u32[]{:S(2)}, u32[]{:S(2)}) async-start(bf16[32,16,8192]{2,1,0:T(8,128)(2,1)} %bitcast.18), calls=%async_computation | async-start | bytes 16777216 | tf_op jit(solution)/shard_map/all_to_all | solution.py:212
  206.5 28.6 %all-to-all-start.1 = ((bf16[32,16,1024]{2,1,0:T(8,128)(2,1)}), bf16[32,16,1024]{2,1,0:T(8,128)(2,1)S(1)}, u32[]{:S(2)}, u32[]{:S(2)}) async-start(bf16[32,16,1024]{2,1,0:T(8,128)(2,1)} %bitcast.21), calls=%async_computation.1 | async-start | bytes 2097152 | tf_op jit(solution)/shard_map/all_to_all | solution.py:234

commit v3 on v2

--- a/solution.py
+++ b/solution.py
@@ -74,7 +74,7 @@
             pl.BlockSpec(memory_space=pltpu.VMEM),
             pl.BlockSpec(memory_space=pltpu.HBM),
         ],
-        out_specs=pl.BlockSpec(memory_space=pltpu.HBM),
+        out_specs=pl.BlockSpec(memory_space=pl.ANY),
         out_shape=jax.ShapeDtypeStruct((slots, width), jnp.bfloat16),
         scratch_shapes=[
             pltpu.VMEM((count, width), jnp.bfloat16),
@@ -100,99 +100,55 @@
 
 
 def term_kernel(
-    adapters,
-    parts,
-    rows_ref,
-    down_ref,
-    up_ref,
-    out_ref,
-    rows_buf,
-    down_buf,
-    up_buf,
-    low_ref,
-    out_buf,
-    rows_sem,
-    down_sem,
-    up_sem,
-    out_sem,
+    adapters, selected_ref, rows_ref, down_ref, up_ref, out_ref, again_ref, out_buf, out_sem
 ):
+    again_ref[...] = selected_ref[...]
     count = rows_ref.shape[0]
     block = count // out_sem.shape[0]
-    last = len(parts) - 1
-
-    def load(k):
-        part = pl.ds(*parts[k])
-        return (
-            pltpu.make_async_copy(down_ref.at[part], down_buf.at[part], down_sem.at[k]),
-            pltpu.make_async_copy(rows_ref.at[:, part], rows_buf.at[:, part], rows_sem.at[k]),
-        )
 
     def store(i):
         part = pl.ds(i * block, block)
         return pltpu.make_async_copy(out_buf.at[part], out_ref.at[part], out_sem.at[i])
 
-    load_up = pltpu.make_async_copy(up_ref, up_buf, up_sem)
-    for k in range(last + 1):
-        for copy in load(k):
-            copy.start()
-    load_up.start()
-    for k, (start, size) in enumerate(parts):
-        for copy in load(k):
-            copy.wait()
-        if k == last:
-            load_up.wait()
-        for i in range(count // block):
-            part = slice(i * block, (i + 1) * block)
-            low = jnp.dot(
-                rows_buf[part, start : start + size],
-                down_buf[start : start + size],
-                preferred_element_type=jnp.float32,
-            )
-            if k > 0:
-                low += low_ref[part]
-            if k < last:
-                low_ref[part] = low
-                continue
-            out_buf[part] = jnp.dot(
-                own_columns(low, adapters), up_buf[...], preferred_element_type=jnp.float32
-            ).astype(jnp.bfloat16)
-            store(i).start()
+    low = lax.dot_general(
+        rows_ref[...], down_ref[...], (((1,), (1,)), ((), ())), preferred_element_type=jnp.float32
+    )
+    low = own_columns(low, adapters)
+    for i in range(count // block):
+        part = slice(i * block, (i + 1) * block)
+        out_buf[part] = jnp.dot(
+            low[part], up_ref[...], preferred_element_type=jnp.float32
+        ).astype(jnp.bfloat16)
+        store(i).start()
     for i in range(count // block):
         store(i).wait()
 
 
-def adapter_terms(rows, down, up, adapters):
+def adapter_terms(selected, rows, down, up, adapters):
     slots, width = rows.shape
     ranks, out_width = up.shape
-    if width % 1024 == 0:
-        eighths = (2, 3, 2, 1)
-        ends = [sum(eighths[: k + 1]) * width // 8 for k in range(4)]
-        parts = [(end - n * width // 8, n * width // 8) for end, n in zip(ends, eighths)]
-    else:
-        parts = [(0, width)]
     return pl.pallas_call(
-        functools.partial(term_kernel, adapters, parts),
-        in_specs=[pl.BlockSpec(memory_space=pltpu.HBM)] * 3,
-        out_specs=pl.BlockSpec(memory_space=pltpu.HBM),
-        out_shape=jax.ShapeDtypeStruct((slots, out_width), jnp.bfloat16),
+        functools.partial(term_kernel, adapters),
+        in_specs=[pl.BlockSpec(memory_space=pltpu.VMEM)] * 4,
+        out_specs=[
+            pl.BlockSpec(memory_space=pltpu.HBM),
+            pl.BlockSpec(memory_space=pltpu.VMEM),
+        ],
+        out_shape=[
+            jax.ShapeDtypeStruct((slots, out_width), jnp.bfloat16),
+            jax.ShapeDtypeStruct(selected.shape, selected.dtype),
+        ],
         scratch_shapes=[
-            pltpu.VMEM((slots, width), jnp.bfloat16),
-            pltpu.VMEM((width, ranks), jnp.bfloat16),
-            pltpu.VMEM((ranks, out_width), jnp.bfloat16),
-            pltpu.VMEM((slots, ranks), jnp.float32),
             pltpu.VMEM((slots, out_width), jnp.bfloat16),
-            pltpu.SemaphoreType.DMA((len(parts),)),
-            pltpu.SemaphoreType.DMA((len(parts),)),
-            pltpu.SemaphoreType.DMA,
             pltpu.SemaphoreType.DMA((2,)),
         ],
-        compiler_params=pltpu.CompilerParams(vmem_limit_bytes=60 * MIB),
+        compiler_params=pltpu.CompilerParams(vmem_limit_bytes=24 * MIB),
         cost_estimate=pl.CostEstimate(
             flops=2 * slots * ranks * (width + out_width),
             bytes_accessed=2 * (slots + ranks) * (width + out_width),
             transcendentals=0,
         ),
-    )(rows, down, up)
+    )(selected, rows, down, up)
 
 
 def per_device(
@@ -210,10 +166,21 @@
 
     outgoing = deal_rows(selected, rows, owners, steps, slots)
     incoming = lax.all_to_all(outgoing, "adapter", split_axis=0, concat_axis=0, tiled=True)
+
+    down = adapter_down_weight.transpose(0, 2, 1).reshape(adapters * rank, width)
+    up = adapter_up_weight.reshape(adapters * rank, out_width)
+    if parts > 1:
+        low = lax.dot_general(
+            incoming, down, (((1,), (1,)), ((), ())), preferred_element_type=jnp.float32
+        )
+        low = own_columns(lax.psum(low, "tensor"), adapters)
+        terms = jnp.dot(low, up, preferred_element_type=jnp.float32).astype(jnp.bfloat16)
+    else:
+        terms, selected = adapter_terms(selected, incoming, down, up, adapters)
+
     base = jnp.dot(rows, key_base_weight, preferred_element_type=jnp.float32)
     if parts > 1:
         base = lax.psum_scatter(base, "tensor", scatter_dimension=1, tiled=True)
-
     position = jnp.arange(requests, dtype=jnp.int32)
     before = (selected.T == selected) & (position[None, :] < position[:, None])
     earlier = jnp.sum(before.astype(jnp.int32), axis=1)
@@ -223,14 +190,6 @@
     deal_back = slot.reshape(-1, 1) == jnp.arange(slots, dtype=jnp.int32)[None, :]
     deal_back = deal_back.astype(jnp.bfloat16)
 
-    down = adapter_down_weight.transpose(1, 0, 2).reshape(width, adapters * rank)
-    up = adapter_up_weight.reshape(adapters * rank, out_width)
-    if parts > 1:
-        low = jnp.dot(incoming, down, preferred_element_type=jnp.float32)
-        low = own_columns(lax.psum(low, "tensor"), adapters)
-        terms = jnp.dot(low, up, preferred_element_type=jnp.float32).astype(jnp.bfloat16)
-    else:
-        terms = adapter_terms(incoming, down, up, adapters)
     returned = lax.all_to_all(terms, "adapter", split_axis=0, concat_axis=0, tiled=True)
     base = lax.optimization_barrier(base)
     own = jnp.dot(deal_back, returned, preferred_element_type=jnp.float32)

time: 238 us -> 234 us (0.983)
  blocking collectives: 0 us -> 190 us
  waiting for transfers between devices: 190 us -> 10.7 us
  local copies, waits for them, and re-layouts: 6.42 us -> 0.02 us
  starting transfers between devices: 10.3 us -> 4.78 us
  Pallas kernels: 13.8 us -> 10.6 us
    all_to_all x0 -> x1, blocking collectives: none -> 190 us  [per_device(): lax.all_to_all(outgoing, 'adapter', split_axis=0, concat_axis=0, tiled=True)]
    all_to_all x1 -> x0, waiting for transfers between devices: 179 us -> none  [per_device(): lax.all_to_all(outgoing, 'adapter', split_axis=0, concat_axis=0, tiled=True)]
    all_to_all x1 -> x0, starting transfers between devices: 7.13 us -> none  [per_device(): lax.all_to_all(outgoing, 'adapter', split_axis=0, concat_axis=0, tiled=True)]
    reshape x1 -> x0, local copies, waits for them, and re-layouts: 6.41 us -> none  [per_device(): adapter_down_weight.transpose(1, 0, 2).reshape(width, adapters * rank)]
    pallas_call x1, Pallas kernels: 7.05 us -> 3.98 us  [adapter_terms(): pl.pallas_call(functools.partial(term_kernel, adapters), in_specs=[pl.Blo...]
  transfers between devices with their start and end apart: 2 -> 1, of which waited for: 2 -> 1; matrix products, arithmetic and copies ran while one was open for 9% -> 6% of each run, Pallas kernels for 0% -> 0%
where the time goes in v3:
time: 234 us; the launch traced here: 232 us
  blocking collectives  190 us (81%)
  matrix products  16 us (7%)
  waiting for transfers between devices  10.7 us (5%)
  Pallas kernels  10.6 us (5%)
  starting transfers between devices  4.78 us (2%)
    all_to_all x1, blocking collectives, per_device(): lax.all_to_all(outgoing, 'adapter', split_axis=0, concat_axis=0, tiled=True)  190 us
    dot_general x1, matrix products, per_device(): base = jnp.dot(rows, key_base_weight, preferred_element_type=jnp.float32)  14.3 us
    all_to_all x1, waiting for transfers between devices, per_device(): lax.all_to_all(terms, 'adapter', split_axis=0, concat_axis=0, tiled=True)  10.7 us
    pallas_call x1, Pallas kernels, deal_rows(): pl.pallas_call(functools.partial(deal_kernel, owners, block), in_specs=[p...  6.64 us
    all_to_all x1, starting transfers between devices, per_device(): lax.all_to_all(terms, 'adapter', split_axis=0, concat_axis=0, tiled=True)  4.78 us
  transfers between devices with their start and end apart: 1, of which 1 were waited for; matrix products, arithmetic and copies ran while one was open for 6% of the time, Pallas kernels for 0%

profile of v3, /device:TPU:1, one launch (start us, length us, event | category | flops | bytes accessed | tf_op | source)
XLA Modules:
  0.0 232.2 jit_solution(5663041981904290878)
XLA Ops:
  0.0 6.6 %shard_map.55 = bf16[512,8192]{1,0:T(8,128)(2,1)} custom-call(s32[1,256]{1,0:T(1,128)} %bitcast.24, bf16[512,8192]{1,0:T(8,128)(2,1)} %bitcast.27), custom_call_target="tpu_custom_call" | custom-call | flops 2147483648 | bytes 16777216 | tf_op jit(solution)/shard_map/pallas_call | solution.py:71
  6.7 0.0 copy-start
  6.7 0.0 copy-start.1
  6.7 0.0 copy-start.2
  6.7 189.7 %all_to_all.23 = bf16[32,16,8192]{2,1,0:T(8,128)(2,1)S(1)} all-to-all(bf16[32,16,8192]{2,1,0:T(8,128)(2,1)} %bitcast.26), channel_id=1, replica_groups=mesh['replica'=1,'adapter'=32,'tensor'=1] {'adapter'}, dimensions={0} | all-to-all | bytes 16777216 | tf_op jit(solution)/shard_map/all_to_all | solution.py:168
  196.4 0.0 copy-done
  196.4 0.0 copy-done.1
  196.4 0.0 copy-done.2
  196.4 4.0 %shard_map.56 = (bf16[512,1024]{1,0:T(8,128)(2,1)}, s32[1,256]{1,0:T(1,128)S(1)}) custom-call(s32[1,256]{1,0:T(1,128)S(1)} %bitcast.25, bf16[512,8192]{1,0:T(8,128)(2,1)S(1)} %bitcast.20, bf16[256,8192]{1,0:T(8,128)(2,1)S(1)} %bitcast.21, bf16[256,1024]{1,0:T(8,128)(2,1)S(1)} %bitcast.22), custom_call_target="tpu_custom_call" | custom-call | flops 2415919104 | bytes 14155776 | tf_op jit(solution)/shard_map/pallas_call | solution.py:130
  200.4 4.8 %all-to-all-start.1 = ((bf16[32,16,1024]{2,1,0:T(8,128)(2,1)}), bf16[32,16,1024]{2,1,0:T(8,128)(2,1)S(1)}, u32[]{:S(2)}, u32[]{:S(2)}) async-start(bf16[32,16,1024]{2,1,0:T(8,128)(2,1)} %bitcast.10), calls=%async_computation.1 | async-start | bytes 2097152 | tf_op jit(solution)/shard_map/all_to_all | solution.py:193
  205.2 14.3 %fusion.3 = f32[512,1024]{1,0:T(8,128)S(1)} fusion(bf16[512,8192]{1,0:T(8,128)(2,1)} %bitcast.28, bf16[8192,1024]{1,0:T(8,128)(2,1)} %param.7), kind=kOutput, calls=%fused_computation.14 | convolution fusion | flops 8589934592 | bytes 27262976 | tf_op jit(solution)/shard_map/dot_general | solution.py:181
  219.5 0.2 convert_reduce_fusion
  219.7 0.1 add_bitcast_fusion
  219.8 10.7 %all-to-all-done.1 = bf16[32,16,1024]{2,1,0:T(8,128)(2,1)S(1)} async-done(((bf16[32,16,1024]{2,1,0:T(8,128)(2,1)}), bf16[32,16,1024]{2,1,0:T(8,128)(2,1)S(1)}, u32[]{:S(2)}, u32[]{:S(2)}) %all-to-all-start.1) | async-done | bytes 1048608 | tf_op jit(solution)/shard_map/all_to_all | solution.py:193
  230.5 1.7 add_convert_fusion
  (3 shorter events, 0.0 us)
Async XLA Ops:
  6.7 189.8 %copy-start = (bf16[4,8192,64]{1,2,0:T(8,128)(2,1)S(1)}, bf16[4,8192,64]{1,2,0:T(8,128)(2,1)}, u32[]{:S(2)}) copy-start(bf16[4,8192,64]{1,2,0:T(8,128)(2,1)} %param.8) | copy-start | bytes 12582916
  6.7 189.7 %copy-start.1 = (bf16[4,64,1024]{2,1,0:T(8,128)(2,1)S(1)}, bf16[4,64,1024]{2,1,0:T(8,128)(2,1)}, u32[]{:S(2)}) copy-start(bf16[4,64,1024]{2,1,0:T(8,128)(2,1)} %param.9) | copy-start | bytes 1572868
  6.7 189.7 %copy-start.2 = (s32[256,1]{0,1:T(1,128)S(1)}, s32[256,1]{0,1:T(1,128)}, u32[]{:S(2)}) copy-start(s32[256,1]{0,1:T(1,128)} %param.6) | copy-start | bytes 3076
  200.4 30.1 %all-to-all-start.1 = ((bf16[32,16,1024]{2,1,0:T(8,128)(2,1)}), bf16[32,16,1024]{2,1,0:T(8,128)(2,1)S(1)}, u32[]{:S(2)}, u32[]{:S(2)}) async-start(bf16[32,16,1024]{2,1,0:T(8,128)(2,1)} %bitcast.10), calls=%async_computation.1 | async-start | bytes 2097152 | tf_op jit(solution)/shard_map/all_to_all | solution.py:193

commit v4 on v3

--- a/solution.py
+++ b/solution.py
@@ -18,7 +18,7 @@
     return block
 
 
-def deal_kernel(owners, block, selected_ref, rows_ref, out_ref, in_buf, out_buf, in_sem, out_sem):
+def deal_kernel(owners, block, selected_ref, rows_ref, out_ref, in_buf, in_sem):
     requests = selected_ref.shape[1]
     count, width = rows_ref.shape
     chunks = width // block
@@ -28,10 +28,6 @@
     def load(k):
         part = pl.ds(k * block, block)
         return pltpu.make_async_copy(rows_ref.at[:, part], in_buf.at[:, part], in_sem.at[k])
-
-    def store(k):
-        part = pl.ds(k * block, block)
-        return pltpu.make_async_copy(out_buf.at[:, part], out_ref.at[:, part], out_sem.at[k])
 
     for k in range(chunks):
         load(k).start()
@@ -57,12 +53,9 @@
             ).reshape(owners, slots // owners, block)
             for step in range(steps)
         ]
-        out_buf[:, part] = (
+        out_ref[:, part] = (
             jnp.concatenate(dealt, axis=1).reshape(slots * steps, block).astype(jnp.bfloat16)
         )
-        store(k).start()
-    for k in range(chunks):
-        store(k).wait()
 
 
 def deal_rows(selected, rows, owners, steps, slots):
@@ -74,15 +67,13 @@
             pl.BlockSpec(memory_space=pltpu.VMEM),
             pl.BlockSpec(memory_space=pltpu.HBM),
         ],
-        out_specs=pl.BlockSpec(memory_space=pl.ANY),
+        out_specs=pl.BlockSpec(memory_space=pltpu.VMEM),
         out_shape=jax.ShapeDtypeStruct((slots, width), jnp.bfloat16),
         scratch_shapes=[
             pltpu.VMEM((count, width), jnp.bfloat16),
-            pltpu.VMEM((slots, width), jnp.bfloat16),
             pltpu.SemaphoreType.DMA((width // block,)),
-            pltpu.SemaphoreType.DMA((width // block,)),
-        ],
-        compiler_params=pltpu.CompilerParams(vmem_limit_bytes=60 * MIB),
+        ],
+        compiler_params=pltpu.CompilerParams(vmem_limit_bytes=44 * MIB),
         cost_estimate=pl.CostEstimate(
             flops=2 * slots * count * width // steps,
             bytes_accessed=2 * (slots + count) * width,

time: 234 us -> 232 us (level)
  no operation moved by 1% of the time
where the time goes in v4:
time: 232 us; the launch traced here: 231 us
  blocking collectives  190 us (82%)
  matrix products  16 us (7%)
  waiting for transfers between devices  10.7 us (5%)
  Pallas kernels  8.47 us (4%)
  starting transfers between devices  4.77 us (2%)
    all_to_all x1, blocking collectives, per_device(): lax.all_to_all(outgoing, 'adapter', split_axis=0, concat_axis=0, tiled=True)  190 us
    dot_general x1, matrix products, per_device(): base = jnp.dot(rows, key_base_weight, preferred_element_type=jnp.float32)  14.3 us
    all_to_all x1, waiting for transfers between devices, per_device(): lax.all_to_all(terms, 'adapter', split_axis=0, concat_axis=0, tiled=True)  10.7 us
    all_to_all x1, starting transfers between devices, per_device(): lax.all_to_all(terms, 'adapter', split_axis=0, concat_axis=0, tiled=True)  4.77 us
  transfers between devices with their start and end apart: 1, of which 1 were waited for; matrix products, arithmetic and copies ran while one was open for 6% of the time, Pallas kernels for 0%

profile of v4, /device:TPU:1, one launch (start us, length us, event | category | flops | bytes accessed | tf_op | source)
XLA Modules:
  0.0 230.6 jit_solution(1491853381500274563)
XLA Ops:
  0.0 0.0 copy-start.2
  0.0 0.7 copy-done.2
  0.7 4.5 %shard_map.55 = bf16[512,8192]{1,0:T(8,128)(2,1)S(1)} custom-call(s32[1,256]{1,0:T(1,128)S(1)} %bitcast.25, bf16[512,8192]{1,0:T(8,128)(2,1)} %bitcast.27), custom_call_target="tpu_custom_call" | custom-call | flops 2147483648 | bytes 16777216 | tf_op jit(solution)/shard_map/pallas_call | solution.py:64
  5.2 0.0 copy-start
  5.2 0.0 copy-start.1
  5.2 189.5 %all_to_all.23 = bf16[32,16,8192]{2,1,0:T(8,128)(2,1)S(1)} all-to-all(bf16[32,16,8192]{2,1,0:T(8,128)(2,1)S(1)} %bitcast.21), channel_id=1, replica_groups=mesh['replica'=1,'adapter'=32,'tensor'=1] {'adapter'}, dimensions={0} | all-to-all | bytes 16777216 | tf_op jit(solution)/shard_map/all_to_all | solution.py:159
  194.7 0.0 copy-done
  194.7 0.0 copy-done.1
  194.7 4.0 %shard_map.56 = (bf16[512,1024]{1,0:T(8,128)(2,1)}, s32[1,256]{1,0:T(1,128)S(1)}) custom-call(s32[1,256]{1,0:T(1,128)S(1)} %bitcast.26, bf16[512,8192]{1,0:T(8,128)(2,1)S(1)} %bitcast.20, bf16[256,8192]{1,0:T(8,128)(2,1)S(1)} %bitcast.22, bf16[256,1024]{1,0:T(8,128)(2,1)S(1)} %bitcast.23), custom_call_target="tpu_custom_call" | custom-call | flops 2415919104 | bytes 14155776 | tf_op jit(solution)/shard_map/pallas_call | solution.py:121
  198.7 4.8 %all-to-all-start.1 = ((bf16[32,16,1024]{2,1,0:T(8,128)(2,1)}), bf16[32,16,1024]{2,1,0:T(8,128)(2,1)S(1)}, u32[]{:S(2)}, u32[]{:S(2)}) async-start(bf16[32,16,1024]{2,1,0:T(8,128)(2,1)} %bitcast.10), calls=%async_computation.1 | async-start | bytes 2097152 | tf_op jit(solution)/shard_map/all_to_all | solution.py:184
  203.5 14.3 %fusion.3 = f32[512,1024]{1,0:T(8,128)S(1)} fusion(bf16[512,8192]{1,0:T(8,128)(2,1)} %bitcast.28, bf16[8192,1024]{1,0:T(8,128)(2,1)} %param.7), kind=kOutput, calls=%fused_computation.14 | convolution fusion | flops 8589934592 | bytes 27262976 | tf_op jit(solution)/shard_map/dot_general | solution.py:172
  217.8 0.2 convert_reduce_fusion
  218.0 0.1 add_bitcast_fusion
  218.1 10.7 %all-to-all-done.1 = bf16[32,16,1024]{2,1,0:T(8,128)(2,1)S(1)} async-done(((bf16[32,16,1024]{2,1,0:T(8,128)(2,1)}), bf16[32,16,1024]{2,1,0:T(8,128)(2,1)S(1)}, u32[]{:S(2)}, u32[]{:S(2)}) %all-to-all-start.1) | async-done | bytes 1048608 | tf_op jit(solution)/shard_map/all_to_all | solution.py:184
  228.8 1.7 add_convert_fusion
  (3 shorter events, 0.0 us)
Async XLA Ops:
  0.0 0.7 copy-start.2
  5.2 189.6 %copy-start = (bf16[4,8192,64]{1,2,0:T(8,128)(2,1)S(1)}, bf16[4,8192,64]{1,2,0:T(8,128)(2,1)}, u32[]{:S(2)}) copy-start(bf16[4,8192,64]{1,2,0:T(8,128)(2,1)} %param.8) | copy-start | bytes 12582916
  5.2 189.5 %copy-start.1 = (bf16[4,64,1024]{2,1,0:T(8,128)(2,1)S(1)}, bf16[4,64,1024]{2,1,0:T(8,128)(2,1)}, u32[]{:S(2)}) copy-start(bf16[4,64,1024]{2,1,0:T(8,128)(2,1)} %param.9) | copy-start | bytes 1572868
  198.7 30.1 %all-to-all-start.1 = ((bf16[32,16,1024]{2,1,0:T(8,128)(2,1)}), bf16[32,16,1024]{2,1,0:T(8,128)(2,1)S(1)}, u32[]{:S(2)}, u32[]{:S(2)}) async-start(bf16[32,16,1024]{2,1,0:T(8,128)(2,1)} %bitcast.10), calls=%async_computation.1 | async-start | bytes 2097152 | tf_op jit(solution)/shard_map/all_to_all | solution.py:184

commit v5 on v4

--- a/solution.py
+++ b/solution.py
@@ -9,6 +9,7 @@
 
 MOST = 2
 MIB = 1 << 20
+PARTS = 8
 
 
 def block_of(width, most):
@@ -18,7 +19,7 @@
     return block
 
 
-def deal_kernel(owners, block, selected_ref, rows_ref, out_ref, in_buf, in_sem):
+def deal_kernel(owners, block, selected_ref, rows_ref, after_ref, out_ref, in_buf, in_sem):
     requests = selected_ref.shape[1]
     count, width = rows_ref.shape
     chunks = width // block
@@ -58,7 +59,7 @@
         )
 
 
-def deal_rows(selected, rows, owners, steps, slots):
+def deal_rows(selected, rows, after, owners, steps, slots):
     count, width = rows.shape
     block = block_of(width, 2048)
     return pl.pallas_call(
@@ -66,6 +67,7 @@
         in_specs=[
             pl.BlockSpec(memory_space=pltpu.VMEM),
             pl.BlockSpec(memory_space=pltpu.HBM),
+            pl.BlockSpec(memory_space=pltpu.HBM),
         ],
         out_specs=pl.BlockSpec(memory_space=pltpu.VMEM),
         out_shape=jax.ShapeDtypeStruct((slots, width), jnp.bfloat16),
@@ -79,7 +81,7 @@
             bytes_accessed=2 * (slots + count) * width,
             transcendentals=0,
         ),
-    )(selected, rows)
+    )(selected, rows, after)
 
 
 def own_columns(low, adapters):
@@ -91,55 +93,96 @@
 
 
 def term_kernel(
-    adapters, selected_ref, rows_ref, down_ref, up_ref, out_ref, again_ref, out_buf, out_sem
+    adapters,
+    side_ref,
+    selected_ref,
+    rows_ref,
+    down_ref,
+    mate_down_ref,
+    up_ref,
+    mate_up_ref,
+    out_ref,
+    again_ref,
+    rows_buf,
+    down_buf,
+    out_buf,
+    rows_sem,
+    down_sem,
+    out_sem,
 ):
     again_ref[...] = selected_ref[...]
-    count = rows_ref.shape[0]
-    block = count // out_sem.shape[0]
-
-    def store(i):
-        part = pl.ds(i * block, block)
-        return pltpu.make_async_copy(out_buf.at[part], out_ref.at[part], out_sem.at[i])
-
-    low = lax.dot_general(
-        rows_ref[...], down_ref[...], (((1,), (1,)), ((), ())), preferred_element_type=jnp.float32
-    )
-    low = own_columns(low, adapters)
-    for i in range(count // block):
-        part = slice(i * block, (i + 1) * block)
-        out_buf[part] = jnp.dot(
-            low[part], up_ref[...], preferred_element_type=jnp.float32
-        ).astype(jnp.bfloat16)
-        store(i).start()
-    for i in range(count // block):
-        store(i).wait()
-
-
-def adapter_terms(selected, rows, down, up, adapters):
-    slots, width = rows.shape
+    chips, _, own_rows, width = rows_ref.shape
+    mine = side_ref[0]
+    sides = (mine, 1 - mine)
+    downs = (down_ref, down_buf)
+    ups = (up_ref, mate_up_ref)
+
+    def pick(turn):
+        return pltpu.make_async_copy(
+            rows_ref.at[:, sides[turn]], rows_buf.at[turn], rows_sem.at[turn]
+        )
+
+    def store(turn):
+        return pltpu.make_async_copy(
+            out_buf.at[turn], out_ref.at[:, sides[turn]], out_sem.at[turn]
+        )
+
+    load = pltpu.make_async_copy(mate_down_ref, down_buf, down_sem)
+    for turn in range(2):
+        pick(turn).start()
+    load.start()
+    for turn in range(2):
+        pick(turn).wait()
+        if turn == 1:
+            load.wait()
+        low = lax.dot_general(
+            rows_buf[turn].reshape(chips * own_rows, width),
+            downs[turn][...],
+            (((1,), (1,)), ((), ())),
+            preferred_element_type=jnp.float32,
+        )
+        term = jnp.dot(
+            own_columns(low, adapters), ups[turn][...], preferred_element_type=jnp.float32
+        )
+        out_buf[turn] = term.astype(jnp.bfloat16).reshape(chips, own_rows, -1)
+        store(turn).start()
+    for turn in range(2):
+        store(turn).wait()
+
+
+def adapter_terms(side, selected, rows, down, mate_down, up, mate_up, adapters):
     ranks, out_width = up.shape
+    width = rows.shape[-1]
+    slots = rows.size // width
     return pl.pallas_call(
         functools.partial(term_kernel, adapters),
-        in_specs=[pl.BlockSpec(memory_space=pltpu.VMEM)] * 4,
+        in_specs=[pl.BlockSpec(memory_space=pltpu.SMEM)]
+        + [pl.BlockSpec(memory_space=pltpu.VMEM)] * 3
+        + [pl.BlockSpec(memory_space=pltpu.HBM)]
+        + [pl.BlockSpec(memory_space=pltpu.VMEM)] * 2,
         out_specs=[
             pl.BlockSpec(memory_space=pltpu.HBM),
             pl.BlockSpec(memory_space=pltpu.VMEM),
         ],
         out_shape=[
-            jax.ShapeDtypeStruct((slots, out_width), jnp.bfloat16),
+            jax.ShapeDtypeStruct(rows.shape[:-1] + (out_width,), jnp.bfloat16),
             jax.ShapeDtypeStruct(selected.shape, selected.dtype),
         ],
         scratch_shapes=[
-            pltpu.VMEM((slots, out_width), jnp.bfloat16),
+            pltpu.VMEM((2, rows.shape[0]) + rows.shape[2:], rows.dtype),
+            pltpu.VMEM(mate_down.shape, mate_down.dtype),
+            pltpu.VMEM((2, rows.shape[0], rows.shape[2], out_width), rows.dtype),
             pltpu.SemaphoreType.DMA((2,)),
-        ],
-        compiler_params=pltpu.CompilerParams(vmem_limit_bytes=24 * MIB),
+            pltpu.SemaphoreType.DMA,
+            pltpu.SemaphoreType.DMA((2,)),
+        ],
+        compiler_params=pltpu.CompilerParams(vmem_limit_bytes=20 * MIB),
         cost_estimate=pl.CostEstimate(
             flops=2 * slots * ranks * (width + out_width),
-            bytes_accessed=2 * (slots + ranks) * (width + out_width),
+            bytes_accessed=2 * (slots + 2 * ranks) * (width + out_width),
             transcendentals=0,
         ),
-    )(selected, rows, down, up)
+    )(side, selected, rows, down, mate_down, up, mate_up)
 
 
 def per_device(
@@ -155,23 +198,59 @@
     rows = hidden.reshape(steps * requests, width)
     selected = request_adapter_index.reshape(1, requests)
 
-    outgoing = deal_rows(selected, rows, owners, steps, slots)
-    incoming = lax.all_to_all(outgoing, "adapter", split_axis=0, concat_axis=0, tiled=True)
-
+    side = lax.axis_index("adapter") % 2
+    mates = [(i, i ^ 1) for i in range(owners)]
+    teams = [list(range(0, owners, 2)), list(range(1, owners, 2))]
     down = adapter_down_weight.transpose(0, 2, 1).reshape(adapters * rank, width)
     up = adapter_up_weight.reshape(adapters * rank, out_width)
+    mate_down = lax.ppermute(down, "adapter", mates)
+    mate_up = lax.ppermute(up, "adapter", mates)
+
+    def base_of_parts():
+        part = width // PARTS
+
+        def add(k, total):
+            return total + jnp.dot(
+                lax.dynamic_slice_in_dim(rows, k * part, part, 1),
+                lax.dynamic_slice_in_dim(key_base_weight, k * part, part, 0),
+                preferred_element_type=jnp.float32,
+            )
+
+        zeros = jnp.zeros((steps * requests, key_base_weight.shape[1]), jnp.float32)
+        return lax.fori_loop(0, PARTS, add, zeros)
+
+    early = lax.cond(
+        side == 1,
+        base_of_parts,
+        lambda: jnp.zeros((steps * requests, key_base_weight.shape[1]), jnp.float32),
+    )
+    outgoing = deal_rows(selected, rows, early, owners, steps, slots)
+    outgoing, mate_down, mate_up = lax.optimization_barrier((outgoing, mate_down, mate_up))
+    incoming = lax.all_to_all(
+        outgoing, "adapter", split_axis=0, concat_axis=0, tiled=True, axis_index_groups=teams
+    )
+    incoming = incoming.reshape(owners // 2, 2, steps * own_slots, width)
     if parts > 1:
-        low = lax.dot_general(
-            incoming, down, (((1,), (1,)), ((), ())), preferred_element_type=jnp.float32
-        )
-        low = own_columns(lax.psum(low, "tensor"), adapters)
-        terms = jnp.dot(low, up, preferred_element_type=jnp.float32).astype(jnp.bfloat16)
+        terms = jnp.zeros(incoming.shape[:-1] + (out_width,), jnp.bfloat16)
+        for turn, (d, u) in enumerate(((down, up), (mate_down, mate_up))):
+            own_side = side if turn == 0 else 1 - side
+            own_in = lax.dynamic_index_in_dim(incoming, own_side, 1, keepdims=False)
+            low = lax.dot_general(
+                own_in.reshape(slots // 2, width),
+                d,
+                (((1,), (1,)), ((), ())),
+                preferred_element_type=jnp.float32,
+            )
+            low = own_columns(lax.psum(low, "tensor"), adapters)
+            term = jnp.dot(low, u, preferred_element_type=jnp.float32).astype(jnp.bfloat16)
+            term = term.reshape(owners // 2, steps * own_slots, out_width)
+            terms = lax.dynamic_update_index_in_dim(terms, term, own_side, 1)
     else:
-        terms, selected = adapter_terms(selected, incoming, down, up, adapters)
-
-    base = jnp.dot(rows, key_base_weight, preferred_element_type=jnp.float32)
-    if parts > 1:
-        base = lax.psum_scatter(base, "tensor", scatter_dimension=1, tiled=True)
+        terms, selected = adapter_terms(
+            side[None], selected, incoming, down, mate_down, up, mate_up, adapters
+        )
+    terms = terms.reshape(slots, out_width)
+
     position = jnp.arange(requests, dtype=jnp.int32)
     before = (selected.T == selected) & (position[None, :] < position[:, None])
     earlier = jnp.sum(before.astype(jnp.int32), axis=1)
@@ -181,9 +260,18 @@
     deal_back = slot.reshape(-1, 1) == jnp.arange(slots, dtype=jnp.int32)[None, :]
     deal_back = deal_back.astype(jnp.bfloat16)
 
-    returned = lax.all_to_all(terms, "adapter", split_axis=0, concat_axis=0, tiled=True)
-    base = lax.optimization_barrier(base)
+    returned = lax.all_to_all(
+        terms, "adapter", split_axis=0, concat_axis=0, tiled=True, axis_index_groups=teams
+    )
     own = jnp.dot(deal_back, returned, preferred_element_type=jnp.float32)
+    late = lax.cond(
+        side == 1,
+        lambda: early,
+        lambda: jnp.dot(rows, key_base_weight, preferred_element_type=jnp.float32),
+    )
+    base = lax.optimization_barrier(late)
+    if parts > 1:
+        base = lax.psum_scatter(base, "tensor", scatter_dimension=1, tiled=True)
     out = (base + own).astype(jnp.bfloat16)
     return out.reshape(steps, requests, out_width)
 

time: 232 us -> 231 us (level)
  blocking collectives: 190 us -> 156 us
  matrix products: 16 us -> 43.8 us
  waiting for transfers between devices: 10.7 us -> 14.7 us
  Pallas kernels: 8.47 us -> 11.2 us
    all_to_all x1, blocking collectives: 190 us -> 156 us  [per_device(): lax.all_to_all(outgoing, 'adapter', split_axis=0, concat_axis=0, tiled=Tr...]
    dot_general x1 -> x8, matrix products: 14.3 us -> 40.5 us  [add(): jnp.dot(lax.dynamic_slice_in_dim(rows, k * part, part, 1), lax.dynamic_sl...]
    all_to_all x1, waiting for transfers between devices: 10.7 us -> 14.7 us  [per_device(): lax.all_to_all(terms, 'adapter', split_axis=0, concat_axis=0, tiled=True,...]
    pallas_call x1, Pallas kernels: 3.98 us -> 6.72 us  [adapter_terms(): pl.pallas_call(functools.partial(term_kernel, adapters), in_specs=[pl.Blo...]
  transfers between devices with their start and end apart: 1 -> 3, of which waited for: 1 -> 1; matrix products, arithmetic and copies ran while one was open for 6% -> 18% of each run, Pallas kernels for 0% -> 2%
where the time goes in v5:
time: 231 us; the launch traced here: 230 us
  blocking collectives  156 us (68%)
  matrix products  43.8 us (19%)
  waiting for transfers between devices  14.7 us (6%)
  Pallas kernels  11.2 us (5%)
  starting transfers between devices  4.22 us (2%)
    all_to_all x1, blocking collectives, per_device(): lax.all_to_all(outgoing, 'adapter', split_axis=0, concat_axis=0, tiled=Tr...  156 us
    dot_general x8, matrix products, add(): jnp.dot(lax.dynamic_slice_in_dim(rows, k * part, part, 1), lax.dynamic_sl...  40.5 us
    all_to_all x1, waiting for transfers between devices, per_device(): lax.all_to_all(terms, 'adapter', split_axis=0, concat_axis=0, tiled=True,...  14.7 us
    pallas_call x1, Pallas kernels, adapter_terms(): pl.pallas_call(functools.partial(term_kernel, adapters), in_specs=[pl.Blo...  6.72 us
  transfers between devices with their start and end apart: 3, of which 1 were waited for; matrix products, arithmetic and copies ran while one was open for 18% of the time, Pallas kernels for 2%

profile of v5, /device:TPU:1, one launch (start us, length us, event | category | flops | bytes accessed | tf_op | source)
XLA Modules:
  0.0 230.4 jit_solution(3511386963300521836)
XLA Ops:
  0.0 0.1 collective-permute-start
  0.1 0.5 collective-permute-start.1
  0.5 40.5 %conditional.2 = (f32[512,1024]{1,0:T(8,128)}) conditional(s32[]{:T(128)} %convert_element_type.11, () %tuple.33, (bf16[512,8192]{1,0:T(8,128)(2,1)}, bf16[8192,1024]{1,0:T(8,128)(2,1)}) %tuple.54), branch_computations={%region_0.1_spmd, %region_1.4_spmd} | conditional | flops 1074790400 | bytes 7341796 | solution.py:222
  0.5 40.5 %while.13 = (s32[]{:T(128)}, f32[512,1024]{1,0:T(8,128)}, bf16[512,8192]{1,0:T(8,128)(2,1)}, bf16[8192,1024]{1,0:T(8,128)(2,1)}, s32[]{:T(128)}, /*index=5*/s32[]{:T(128)}, s32[]{:T(128)}, s32[]{:T(128)}) while((s32[]{:T(128)}, f32[512,1024]{1,0:T(8,128)}, bf16[512,8192]{1,0:T(8,128)(2,1)}, bf16[8192,1024]{1,0:T(8,128)(2,1)}, ...), condition=%wide.region_3.3_spmd.clone, body=%wide.region_2.2_spmd.clone.sunk | while | flops 1074790400 | bytes 7341716 | solution.py:220
  0.5 4.5 %select_add_fusion.2 = f32[512,1024]{1,0:T(8,128)} fusion(f32[512,1024]{1,0:T(8,128)} %get-tuple-element.170, bf16[8192,1024]{1,0:T(8,128)(2,1)} %get-tuple-element.180, s32[]{:T(128)S(6)} %select_n.39, bf16[512,8192]{1,0:T(8,128)(2,1)} %get-tuple-element.179, pred[]{:T(512)S(6)} %compare.9), kind=kOutput, calls=%fused_computation.clone.1 | convolution fusion | flops 1074790400 | bytes 7341568 | tf_op jit(solution)/shard_map/cond/branch_1_fun/while/body/eval_jaxpr/dot_general | solution.py:213
  5.0 5.1 %select_add_fusion.2 = f32[512,1024]{1,0:T(8,128)} fusion(f32[512,1024]{1,0:T(8,128)} %get-tuple-element.170, bf16[8192,1024]{1,0:T(8,128)(2,1)} %get-tuple-element.180, s32[]{:T(128)S(6)} %select_n.39, bf16[512,8192]{1,0:T(8,128)(2,1)} %get-tuple-element.179, pred[]{:T(512)S(6)} %compare.9), kind=kOutput, calls=%fused_computation.clone.1 | convolution fusion | flops 1074790400 | bytes 7341568 | tf_op jit(solution)/shard_map/cond/branch_1_fun/while/body/eval_jaxpr/dot_general | solution.py:213
  10.2 5.1 %select_add_fusion.2 = f32[512,1024]{1,0:T(8,128)} fusion(f32[512,1024]{1,0:T(8,128)} %get-tuple-element.170, bf16[8192,1024]{1,0:T(8,128)(2,1)} %get-tuple-element.180, s32[]{:T(128)S(6)} %select_n.39, bf16[512,8192]{1,0:T(8,128)(2,1)} %get-tuple-element.179, pred[]{:T(512)S(6)} %compare.9), kind=kOutput, calls=%fused_computation.clone.1 | convolution fusion | flops 1074790400 | bytes 7341568 | tf_op jit(solution)/shard_map/cond/branch_1_fun/while/body/eval_jaxpr/dot_general | solution.py:213
  15.3 5.1 %select_add_fusion.2 = f32[512,1024]{1,0:T(8,128)} fusion(f32[512,1024]{1,0:T(8,128)} %get-tuple-element.170, bf16[8192,1024]{1,0:T(8,128)(2,1)} %get-tuple-element.180, s32[]{:T(128)S(6)} %select_n.39, bf16[512,8192]{1,0:T(8,128)(2,1)} %get-tuple-element.179, pred[]{:T(512)S(6)} %compare.9), kind=kOutput, calls=%fused_computation.clone.1 | convolution fusion | flops 1074790400 | bytes 7341568 | tf_op jit(solution)/shard_map/cond/branch_1_fun/while/body/eval_jaxpr/dot_general | solution.py:213
  20.5 5.1 %select_add_fusion.2 = f32[512,1024]{1,0:T(8,128)} fusion(f32[512,1024]{1,0:T(8,128)} %get-tuple-element.170, bf16[8192,1024]{1,0:T(8,128)(2,1)} %get-tuple-element.180, s32[]{:T(128)S(6)} %select_n.39, bf16[512,8192]{1,0:T(8,128)(2,1)} %get-tuple-element.179, pred[]{:T(512)S(6)} %compare.9), kind=kOutput, calls=%fused_computation.clone.1 | convolution fusion | flops 1074790400 | bytes 7341568 | tf_op jit(solution)/shard_map/cond/branch_1_fun/while/body/eval_jaxpr/dot_general | solution.py:213
  25.6 5.1 %select_add_fusion.2 = f32[512,1024]{1,0:T(8,128)} fusion(f32[512,1024]{1,0:T(8,128)} %get-tuple-element.170, bf16[8192,1024]{1,0:T(8,128)(2,1)} %get-tuple-element.180, s32[]{:T(128)S(6)} %select_n.39, bf16[512,8192]{1,0:T(8,128)(2,1)} %get-tuple-element.179, pred[]{:T(512)S(6)} %compare.9), kind=kOutput, calls=%fused_computation.clone.1 | convolution fusion | flops 1074790400 | bytes 7341568 | tf_op jit(solution)/shard_map/cond/branch_1_fun/while/body/eval_jaxpr/dot_general | solution.py:213
  30.7 5.1 %select_add_fusion.2 = f32[512,1024]{1,0:T(8,128)} fusion(f32[512,1024]{1,0:T(8,128)} %get-tuple-element.170, bf16[8192,1024]{1,0:T(8,128)(2,1)} %get-tuple-element.180, s32[]{:T(128)S(6)} %select_n.39, bf16[512,8192]{1,0:T(8,128)(2,1)} %get-tuple-element.179, pred[]{:T(512)S(6)} %compare.9), kind=kOutput, calls=%fused_computation.clone.1 | convolution fusion | flops 1074790400 | bytes 7341568 | tf_op jit(solution)/shard_map/cond/branch_1_fun/while/body/eval_jaxpr/dot_general | solution.py:213
  35.9 5.1 %select_add_fusion.2 = f32[512,1024]{1,0:T(8,128)} fusion(f32[512,1024]{1,0:T(8,128)} %get-tuple-element.170, bf16[8192,1024]{1,0:T(8,128)(2,1)} %get-tuple-element.180, s32[]{:T(128)S(6)} %select_n.39, bf16[512,8192]{1,0:T(8,128)(2,1)} %get-tuple-element.179, pred[]{:T(512)S(6)} %compare.9), kind=kOutput, calls=%fused_computation.clone.1 | convolution fusion | flops 1074790400 | bytes 7341568 | tf_op jit(solution)/shard_map/cond/branch_1_fun/while/body/eval_jaxpr/dot_general | solution.py:213
  41.0 4.5 %shard_map.55 = bf16[512,8192]{1,0:T(8,128)(2,1)S(1)} custom-call(s32[1,256]{1,0:T(1,128)S(1)} %bitcast.28, bf16[512,8192]{1,0:T(8,128)(2,1)} %bitcast.31, f32[512,1024]{1,0:T(8,128)} %get-tuple-element.185.after_ref), custom_call_target="tpu_custom_call" | custom-call | flops 2147483648 | bytes 16777216 | tf_op jit(solution)/shard_map/pallas_call | solution.py:65
  45.5 0.0 collective-permute-done.1.mate_up_ref
  45.5 0.0 collective-permute-done.mate_down_ref
  45.6 0.0 copy-start
  45.6 0.0 copy-start.1
  45.6 156.0 %all_to_all.21 = bf16[16,32,8192]{2,1,0:T(8,128)(2,1)S(1)} all-to-all(bf16[16,32,8192]{2,1,0:T(8,128)(2,1)S(1)} %bitcast.21), channel_id=1, replica_groups={{0,2,4,6,8,10,12,14,16,18,20,22,24,26,28,30},{1,3,5,7,9,11,13,15,17,19,..., dimensions={0} | all-to-all | bytes 16777216 | tf_op jit(solution)/shard_map/all_to_all | solution.py:229
  201.6 6.7 %shard_map.56 = (bf16[16,2,16,1024]{3,2,1,0:T(8,128)(2,1)}, s32[1,256]{1,0:T(1,128)S(1)}) custom-call(s32[1]{0:T(128)} %bitcast.1.side_ref, s32[1,256]{1,0:T(1,128)S(1)} %bitcast.29, bf16[16,2,16,8192]{3,2,1,0:T(8,128)(2,1)S(1)} %bitcast.22, bf16[256,8192]{1,0:T(8,128)(2,1)S(1)} %bitcast.24, bf16[256,8192]{1,0:T(8,128)(2,1)} %collective-permute-done.mate_down_ref, ...), custom_call_target="tpu_custom_call" | custom-call | flops 2415919104 | bytes 18874368 | tf_op jit(solution)/shard_map/pallas_call | solution.py:157
  208.3 3.7 %all-to-all-start.1 = ((bf16[16,32,1024]{2,1,0:T(8,128)(2,1)}), bf16[16,32,1024]{2,1,0:T(8,128)(2,1)S(1)}, u32[]{:S(2)}, u32[]{:S(2)}) async-start(bf16[16,32,1024]{2,1,0:T(8,128)(2,1)} %bitcast.11), calls=%async_computation.1 | async-start | bytes 2097152 | tf_op jit(solution)/shard_map/all_to_all | solution.py:263
  212.1 0.2 convert_reduce_fusion
  212.3 0.1 add_bitcast_fusion
  212.4 14.7 %all-to-all-done.1 = bf16[16,32,1024]{2,1,0:T(8,128)(2,1)S(1)} async-done(((bf16[16,32,1024]{2,1,0:T(8,128)(2,1)}), bf16[16,32,1024]{2,1,0:T(8,128)(2,1)S(1)}, u32[]{:S(2)}, u32[]{:S(2)}) %all-to-all-start.1) | async-done | bytes 1048608 | tf_op jit(solution)/shard_map/all_to_all | solution.py:263
  227.1 3.3 %add_convert_fusion = bf16[512,1024]{1,0:T(8,128)(2,1)} fusion(f32[512,1024]{1,0:T(8,128)} %get-tuple-element.186, bf16[512,1024]{1,0:T(8,128)(2,1)S(1)} %bitcast.33, s32[512]{0:T(512)S(1)} %bitcast.34), kind=kOutput, calls=%fused_computation.5 | convolution fusion | flops 538181632 | bytes 4196352 | tf_op jit(solution)/shard_map/dot_general | solution.py:266
  (9 shorter events, 0.1 us)
Async XLA Ops:
  0.0 45.5 %collective-permute-start = (bf16[256,8192]{1,0:T(8,128)(2,1)}, bf16[256,8192]{1,0:T(8,128)(2,1)}, u32[]{:S(2)}, u32[]{:S(2)}) collective-permute-start(bf16[256,8192]{1,0:T(8,128)(2,1)} %bitcast.23), channel_id=1, source_target_pairs={{0,1},{1,0},{2,3},{3,2},{4,5},{5,4},{6,7},{7,6},{8,9},{9,8},{10,11... | collective-permute-start | bytes 12582920 | tf_op jit(solution)/shard_map/ppermute | solution.py:206
  0.1 45.5 %collective-permute-start.1 = (bf16[256,1024]{1,0:T(8,128)(2,1)}, bf16[256,1024]{1,0:T(8,128)(2,1)S(1)}, u32[]{:S(2)}, u32[]{:S(2)}) collective-permute-start(bf16[256,1024]{1,0:T(8,128)(2,1)} %bitcast.25), channel_id=1, source_target_pairs={{0,1},{1,0},{2,3},{3,2},{4,5},{5,4},{6,7},{7,6},{8,9},{9,8},{10,11... | collective-permute-start | bytes 1572872 | tf_op jit(solution)/shard_map/ppermute | solution.py:207
  0.5 40.5 %copy-start.2 = (s32[256,1]{0,1:T(1,128)S(1)}, s32[256,1]{0,1:T(1,128)}, u32[]{:S(2)}) copy-start(s32[256,1]{0,1:T(1,128)} %param.12) | copy-start | bytes 3076
  45.6 156.0 %copy-start = (bf16[4,8192,64]{1,2,0:T(8,128)(2,1)S(1)}, bf16[4,8192,64]{1,2,0:T(8,128)(2,1)}, u32[]{:S(2)}) copy-start(bf16[4,8192,64]{1,2,0:T(8,128)(2,1)} %param.14) | copy-start | bytes 12582916
  45.6 156.0 %copy-start.1 = (bf16[4,64,1024]{2,1,0:T(8,128)(2,1)S(1)}, bf16[4,64,1024]{2,1,0:T(8,128)(2,1)}, u32[]{:S(2)}) copy-start(bf16[4,64,1024]{2,1,0:T(8,128)(2,1)} %param.15) | copy-start | bytes 1572868
  208.3 18.8 %all-to-all-start.1 = ((bf16[16,32,1024]{2,1,0:T(8,128)(2,1)}), bf16[16,32,1024]{2,1,0:T(8,128)(2,1)S(1)}, u32[]{:S(2)}, u32[]{:S(2)}) async-start(bf16[16,32,1024]{2,1,0:T(8,128)(2,1)} %bitcast.11), calls=%async_computation.1 | async-start | bytes 2097152 | tf_op jit(solution)/shard_map/all_to_all | solution.py:263

commit v6 on v5

--- a/solution.py
+++ b/solution.py
@@ -103,10 +103,8 @@
     mate_up_ref,
     out_ref,
     again_ref,
-    rows_buf,
     down_buf,
     out_buf,
-    rows_sem,
     down_sem,
     out_sem,
 ):
@@ -117,26 +115,17 @@
     downs = (down_ref, down_buf)
     ups = (up_ref, mate_up_ref)
 
-    def pick(turn):
-        return pltpu.make_async_copy(
-            rows_ref.at[:, sides[turn]], rows_buf.at[turn], rows_sem.at[turn]
-        )
-
     def store(turn):
         return pltpu.make_async_copy(
             out_buf.at[turn], out_ref.at[:, sides[turn]], out_sem.at[turn]
         )
 
     load = pltpu.make_async_copy(mate_down_ref, down_buf, down_sem)
-    for turn in range(2):
-        pick(turn).start()
     load.start()
-    for turn in range(2):
-        pick(turn).wait()
-        if turn == 1:
-            load.wait()
+
+    def add_terms(turn, side):
         low = lax.dot_general(
-            rows_buf[turn].reshape(chips * own_rows, width),
+            rows_ref[:, side].reshape(chips * own_rows, width),
             downs[turn][...],
             (((1,), (1,)), ((), ())),
             preferred_element_type=jnp.float32,
@@ -146,6 +135,12 @@
         )
         out_buf[turn] = term.astype(jnp.bfloat16).reshape(chips, own_rows, -1)
         store(turn).start()
+
+    for turn in range(2):
+        if turn == 1:
+            load.wait()
+        for side in range(2):
+            pl.when(mine == (side + turn) % 2)(functools.partial(add_terms, turn, side))
     for turn in range(2):
         store(turn).wait()
 
@@ -169,10 +164,8 @@
             jax.ShapeDtypeStruct(selected.shape, selected.dtype),
         ],
         scratch_shapes=[
-            pltpu.VMEM((2, rows.shape[0]) + rows.shape[2:], rows.dtype),
             pltpu.VMEM(mate_down.shape, mate_down.dtype),
             pltpu.VMEM((2, rows.shape[0], rows.shape[2], out_width), rows.dtype),
-            pltpu.SemaphoreType.DMA((2,)),
             pltpu.SemaphoreType.DMA,
             pltpu.SemaphoreType.DMA((2,)),
         ],

time: 231 us -> 229 us (level)
  no operation moved by 1% of the time
where the time goes in v6:
time: 229 us; the launch traced here: 228 us
  blocking collectives  156 us (68%)
  matrix products  43.8 us (19%)
  waiting for transfers between devices  14.8 us (6%)
  Pallas kernels  9.23 us (4%)
  starting transfers between devices  4.22 us (2%)
    all_to_all x1, blocking collectives, per_device(): lax.all_to_all(outgoing, 'adapter', split_axis=0, concat_axis=0, tiled=Tr...  156 us
    dot_general x8, matrix products, add(): jnp.dot(lax.dynamic_slice_in_dim(rows, k * part, part, 1), lax.dynamic_sl...  40.5 us
    all_to_all x1, waiting for transfers between devices, per_device(): lax.all_to_all(terms, 'adapter', split_axis=0, concat_axis=0, tiled=True,...  14.7 us
    pallas_call x1, Pallas kernels, adapter_terms(): pl.pallas_call(functools.partial(term_kernel, adapters), in_specs=[pl.Blo...  4.74 us
  transfers between devices with their start and end apart: 3, of which 1 were waited for; matrix products, arithmetic and copies ran while one was open for 18% of the time, Pallas kernels for 2%

profile of v6, /device:TPU:1, one launch (start us, length us, event | category | flops | bytes accessed | tf_op | source)
XLA Modules:
  0.0 228.5 jit_solution(11542645988080436163)
XLA Ops:
  0.0 0.1 collective-permute-start
  0.1 0.5 collective-permute-start.1
  0.5 40.5 %conditional.2 = (f32[512,1024]{1,0:T(8,128)}) conditional(s32[]{:T(128)} %convert_element_type.11, () %tuple.33, (bf16[512,8192]{1,0:T(8,128)(2,1)}, bf16[8192,1024]{1,0:T(8,128)(2,1)}) %tuple.54), branch_computations={%region_0.1_spmd, %region_1.4_spmd} | conditional | flops 1074790400 | bytes 7341796 | solution.py:215
  0.5 40.5 %while.13 = (s32[]{:T(128)}, f32[512,1024]{1,0:T(8,128)}, bf16[512,8192]{1,0:T(8,128)(2,1)}, bf16[8192,1024]{1,0:T(8,128)(2,1)}, s32[]{:T(128)}, /*index=5*/s32[]{:T(128)}, s32[]{:T(128)}, s32[]{:T(128)}) while((s32[]{:T(128)}, f32[512,1024]{1,0:T(8,128)}, bf16[512,8192]{1,0:T(8,128)(2,1)}, bf16[8192,1024]{1,0:T(8,128)(2,1)}, ...), condition=%wide.region_3.3_spmd.clone, body=%wide.region_2.2_spmd.clone.sunk | while | flops 1074790400 | bytes 7341716 | solution.py:213
  0.5 4.5 %select_add_fusion.2 = f32[512,1024]{1,0:T(8,128)} fusion(f32[512,1024]{1,0:T(8,128)} %get-tuple-element.170, bf16[8192,1024]{1,0:T(8,128)(2,1)} %get-tuple-element.180, s32[]{:T(128)S(6)} %select_n.39, bf16[512,8192]{1,0:T(8,128)(2,1)} %get-tuple-element.179, pred[]{:T(512)S(6)} %compare.9), kind=kOutput, calls=%fused_computation.clone.1 | convolution fusion | flops 1074790400 | bytes 7341568 | tf_op jit(solution)/shard_map/cond/branch_1_fun/while/body/eval_jaxpr/dot_general | solution.py:206
  5.0 5.1 %select_add_fusion.2 = f32[512,1024]{1,0:T(8,128)} fusion(f32[512,1024]{1,0:T(8,128)} %get-tuple-element.170, bf16[8192,1024]{1,0:T(8,128)(2,1)} %get-tuple-element.180, s32[]{:T(128)S(6)} %select_n.39, bf16[512,8192]{1,0:T(8,128)(2,1)} %get-tuple-element.179, pred[]{:T(512)S(6)} %compare.9), kind=kOutput, calls=%fused_computation.clone.1 | convolution fusion | flops 1074790400 | bytes 7341568 | tf_op jit(solution)/shard_map/cond/branch_1_fun/while/body/eval_jaxpr/dot_general | solution.py:206
  10.2 5.1 %select_add_fusion.2 = f32[512,1024]{1,0:T(8,128)} fusion(f32[512,1024]{1,0:T(8,128)} %get-tuple-element.170, bf16[8192,1024]{1,0:T(8,128)(2,1)} %get-tuple-element.180, s32[]{:T(128)S(6)} %select_n.39, bf16[512,8192]{1,0:T(8,128)(2,1)} %get-tuple-element.179, pred[]{:T(512)S(6)} %compare.9), kind=kOutput, calls=%fused_computation.clone.1 | convolution fusion | flops 1074790400 | bytes 7341568 | tf_op jit(solution)/shard_map/cond/branch_1_fun/while/body/eval_jaxpr/dot_general | solution.py:206
  15.3 5.1 %select_add_fusion.2 = f32[512,1024]{1,0:T(8,128)} fusion(f32[512,1024]{1,0:T(8,128)} %get-tuple-element.170, bf16[8192,1024]{1,0:T(8,128)(2,1)} %get-tuple-element.180, s32[]{:T(128)S(6)} %select_n.39, bf16[512,8192]{1,0:T(8,128)(2,1)} %get-tuple-element.179, pred[]{:T(512)S(6)} %compare.9), kind=kOutput, calls=%fused_computation.clone.1 | convolution fusion | flops 1074790400 | bytes 7341568 | tf_op jit(solution)/shard_map/cond/branch_1_fun/while/body/eval_jaxpr/dot_general | solution.py:206
  20.5 5.1 %select_add_fusion.2 = f32[512,1024]{1,0:T(8,128)} fusion(f32[512,1024]{1,0:T(8,128)} %get-tuple-element.170, bf16[8192,1024]{1,0:T(8,128)(2,1)} %get-tuple-element.180, s32[]{:T(128)S(6)} %select_n.39, bf16[512,8192]{1,0:T(8,128)(2,1)} %get-tuple-element.179, pred[]{:T(512)S(6)} %compare.9), kind=kOutput, calls=%fused_computation.clone.1 | convolution fusion | flops 1074790400 | bytes 7341568 | tf_op jit(solution)/shard_map/cond/branch_1_fun/while/body/eval_jaxpr/dot_general | solution.py:206
  25.6 5.1 %select_add_fusion.2 = f32[512,1024]{1,0:T(8,128)} fusion(f32[512,1024]{1,0:T(8,128)} %get-tuple-element.170, bf16[8192,1024]{1,0:T(8,128)(2,1)} %get-tuple-element.180, s32[]{:T(128)S(6)} %select_n.39, bf16[512,8192]{1,0:T(8,128)(2,1)} %get-tuple-element.179, pred[]{:T(512)S(6)} %compare.9), kind=kOutput, calls=%fused_computation.clone.1 | convolution fusion | flops 1074790400 | bytes 7341568 | tf_op jit(solution)/shard_map/cond/branch_1_fun/while/body/eval_jaxpr/dot_general | solution.py:206
  30.7 5.1 %select_add_fusion.2 = f32[512,1024]{1,0:T(8,128)} fusion(f32[512,1024]{1,0:T(8,128)} %get-tuple-element.170, bf16[8192,1024]{1,0:T(8,128)(2,1)} %get-tuple-element.180, s32[]{:T(128)S(6)} %select_n.39, bf16[512,8192]{1,0:T(8,128)(2,1)} %get-tuple-element.179, pred[]{:T(512)S(6)} %compare.9), kind=kOutput, calls=%fused_computation.clone.1 | convolution fusion | flops 1074790400 | bytes 7341568 | tf_op jit(solution)/shard_map/cond/branch_1_fun/while/body/eval_jaxpr/dot_general | solution.py:206
  35.9 5.1 %select_add_fusion.2 = f32[512,1024]{1,0:T(8,128)} fusion(f32[512,1024]{1,0:T(8,128)} %get-tuple-element.170, bf16[8192,1024]{1,0:T(8,128)(2,1)} %get-tuple-element.180, s32[]{:T(128)S(6)} %select_n.39, bf16[512,8192]{1,0:T(8,128)(2,1)} %get-tuple-element.179, pred[]{:T(512)S(6)} %compare.9), kind=kOutput, calls=%fused_computation.clone.1 | convolution fusion | flops 1074790400 | bytes 7341568 | tf_op jit(solution)/shard_map/cond/branch_1_fun/while/body/eval_jaxpr/dot_general | solution.py:206
  41.0 4.5 %shard_map.55 = bf16[512,8192]{1,0:T(8,128)(2,1)S(1)} custom-call(s32[1,256]{1,0:T(1,128)S(1)} %bitcast.28, bf16[512,8192]{1,0:T(8,128)(2,1)} %bitcast.31, f32[512,1024]{1,0:T(8,128)} %get-tuple-element.185.after_ref), custom_call_target="tpu_custom_call" | custom-call | flops 2147483648 | bytes 16777216 | tf_op jit(solution)/shard_map/pallas_call | solution.py:65
  45.5 0.0 collective-permute-done.1.mate_up_ref
  45.5 0.0 collective-permute-done.mate_down_ref
  45.6 0.0 copy-start
  45.6 0.0 copy-start.1
  45.6 156.0 %all_to_all.21 = bf16[16,32,8192]{2,1,0:T(8,128)(2,1)S(1)} all-to-all(bf16[16,32,8192]{2,1,0:T(8,128)(2,1)S(1)} %bitcast.21), channel_id=1, replica_groups={{0,2,4,6,8,10,12,14,16,18,20,22,24,26,28,30},{1,3,5,7,9,11,13,15,17,19,..., dimensions={0} | all-to-all | bytes 16777216 | tf_op jit(solution)/shard_map/all_to_all | solution.py:222
  201.6 4.7 %shard_map.56 = (bf16[16,2,16,1024]{3,2,1,0:T(8,128)(2,1)}, s32[1,256]{1,0:T(1,128)S(1)}) custom-call(s32[1]{0:T(128)} %bitcast.1.side_ref, s32[1,256]{1,0:T(1,128)S(1)} %bitcast.29, bf16[16,2,16,8192]{3,2,1,0:T(8,128)(2,1)S(1)} %bitcast.22, bf16[256,8192]{1,0:T(8,128)(2,1)S(1)} %bitcast.24, bf16[256,8192]{1,0:T(8,128)(2,1)} %collective-permute-done.mate_down_ref, ...), custom_call_target="tpu_custom_call" | custom-call | flops 2415919104 | bytes 18874368 | tf_op jit(solution)/shard_map/pallas_call | solution.py:152
  206.4 3.7 %all-to-all-start.1 = ((bf16[16,32,1024]{2,1,0:T(8,128)(2,1)}), bf16[16,32,1024]{2,1,0:T(8,128)(2,1)S(1)}, u32[]{:S(2)}, u32[]{:S(2)}) async-start(bf16[16,32,1024]{2,1,0:T(8,128)(2,1)} %bitcast.11), calls=%async_computation.1 | async-start | bytes 2097152 | tf_op jit(solution)/shard_map/all_to_all | solution.py:256
  210.1 0.2 convert_reduce_fusion
  210.3 0.1 add_bitcast_fusion
  210.4 14.7 %all-to-all-done.1 = bf16[16,32,1024]{2,1,0:T(8,128)(2,1)S(1)} async-done(((bf16[16,32,1024]{2,1,0:T(8,128)(2,1)}), bf16[16,32,1024]{2,1,0:T(8,128)(2,1)S(1)}, u32[]{:S(2)}, u32[]{:S(2)}) %all-to-all-start.1) | async-done | bytes 1048608 | tf_op jit(solution)/shard_map/all_to_all | solution.py:256
  225.1 3.3 %add_convert_fusion = bf16[512,1024]{1,0:T(8,128)(2,1)} fusion(f32[512,1024]{1,0:T(8,128)} %get-tuple-element.186, bf16[512,1024]{1,0:T(8,128)(2,1)S(1)} %bitcast.33, s32[512]{0:T(512)S(1)} %bitcast.34), kind=kOutput, calls=%fused_computation.5 | convolution fusion | flops 538181632 | bytes 4196352 | tf_op jit(solution)/shard_map/dot_general | solution.py:259
  (9 shorter events, 0.1 us)
Async XLA Ops:
  0.0 45.5 %collective-permute-start = (bf16[256,8192]{1,0:T(8,128)(2,1)}, bf16[256,8192]{1,0:T(8,128)(2,1)}, u32[]{:S(2)}, u32[]{:S(2)}) collective-permute-start(bf16[256,8192]{1,0:T(8,128)(2,1)} %bitcast.23), channel_id=1, source_target_pairs={{0,1},{1,0},{2,3},{3,2},{4,5},{5,4},{6,7},{7,6},{8,9},{9,8},{10,11... | collective-permute-start | bytes 12582920 | tf_op jit(solution)/shard_map/ppermute | solution.py:199
  0.1 45.5 %collective-permute-start.1 = (bf16[256,1024]{1,0:T(8,128)(2,1)}, bf16[256,1024]{1,0:T(8,128)(2,1)S(1)}, u32[]{:S(2)}, u32[]{:S(2)}) collective-permute-start(bf16[256,1024]{1,0:T(8,128)(2,1)} %bitcast.25), channel_id=1, source_target_pairs={{0,1},{1,0},{2,3},{3,2},{4,5},{5,4},{6,7},{7,6},{8,9},{9,8},{10,11... | collective-permute-start | bytes 1572872 | tf_op jit(solution)/shard_map/ppermute | solution.py:200
  0.5 40.5 %copy-start.2 = (s32[256,1]{0,1:T(1,128)S(1)}, s32[256,1]{0,1:T(1,128)}, u32[]{:S(2)}) copy-start(s32[256,1]{0,1:T(1,128)} %param.12) | copy-start | bytes 3076
  45.6 156.0 %copy-start = (bf16[4,8192,64]{1,2,0:T(8,128)(2,1)S(1)}, bf16[4,8192,64]{1,2,0:T(8,128)(2,1)}, u32[]{:S(2)}) copy-start(bf16[4,8192,64]{1,2,0:T(8,128)(2,1)} %param.14) | copy-start | bytes 12582916
  45.6 156.0 %copy-start.1 = (bf16[4,64,1024]{2,1,0:T(8,128)(2,1)S(1)}, bf16[4,64,1024]{2,1,0:T(8,128)(2,1)}, u32[]{:S(2)}) copy-start(bf16[4,64,1024]{2,1,0:T(8,128)(2,1)} %param.15) | copy-start | bytes 1572868
  206.4 18.8 %all-to-all-start.1 = ((bf16[16,32,1024]{2,1,0:T(8,128)(2,1)}), bf16[16,32,1024]{2,1,0:T(8,128)(2,1)S(1)}, u32[]{:S(2)}, u32[]{:S(2)}) async-start(bf16[16,32,1024]{2,1,0:T(8,128)(2,1)} %bitcast.11), calls=%async_computation.1 | async-start | bytes 2097152 | tf_op jit(solution)/shard_map/all_to_all | solution.py:256
